TPU v7x, 32 devices: a whole 2x2x4 slice. The times are simulated.
32 devices in a mesh: blk: 2 (over core), team: 16 (over z, y, x).
Axes of the slice: x: 2, y: 2, z: 4, core: 2. Of those that a mesh axis runs over, the one named last changes fastest.
Arguments:
- features: bfloat16 [4096, 256], P(('blk', 'team')), may hold values from -6 to 6
- weight: bfloat16 [256, 256], replicated, may hold values from -0.375 to 0.375
- bias: float32 [256], replicated, may hold values from -3 to 3
- cotangent: bfloat16 [4096, 256], P(('blk', 'team')), may hold values from -6 to 6
- adj_cols: int32 [16, 2, 2, 12], P('team', None, 'blk'), may hold values from 0 to 15, as said below
- adj_vals: bfloat16 [16, 2, 2, 12, 128, 128], P('team', None, 'blk'), as said below
Outputs:
- hidden: bfloat16 [4096, 256], P(('blk', 'team'))
- grad_input: bfloat16 [4096, 256], P(('blk', 'team'))
- grad_weight: float32 [256, 256], replicated
- grad_bias: float32 [256], replicated
Inputs may be any that keep to these rules, and one draw needn't show every extreme that they name: `adj_cols`: for every node panel and column group the 12 entries are distinct. Block (i, j) of A is listed exactly when block (j, i) is, every column panel is listed by exactly 12 row panels of each column group, and A is symmetric. `adj_vals`: the block listed for panels (i, j) is the transpose of the block listed for (j, i), so A is symmetric.
All inputs are finite; a program needn't handle non-finite values.
Results may differ from a plain program's by a relative error of at most 0.0075.
Values may be sent and summed in bfloat16 or wider, within the bound.
A program may use at most 64 MiB of HBM per device.

v0:
```python
import jax
import jax.numpy as jnp
from jax import lax
from jax.sharding import PartitionSpec as P


def collect(panels, adj_cols, adj_vals):
    block = adj_vals.shape[-1]
    width = panels.shape[1]
    stacked = panels.reshape(panels.shape[0] // block, block, width)
    picked = jnp.take(stacked, adj_cols[0, :, 0, :], axis=0)
    summed = jnp.einsum(
        "rkij,rkjf->rif", adj_vals[0, :, 0], picked, preferred_element_type=jnp.float32
    )
    return summed.reshape(-1, width)


def activation(value):
    return jax.nn.gelu(value, approximate=True)


def local(features, weight, bias, cotangent, adj_cols, adj_vals):
    gathered = jnp.dot(
        lax.all_gather(features, "team", axis=0, tiled=True),
        weight,
        preferred_element_type=jnp.float32,
    ).astype(jnp.bfloat16)
    partial_rows = collect(gathered, adj_cols, adj_vals)
    summed = lax.psum_scatter(partial_rows, "blk", scatter_dimension=0, tiled=True)
    pre = summed + bias[None, :]
    activated, pullback = jax.vjp(activation, pre)
    hidden = activated.astype(jnp.bfloat16)
    pulled = pullback(cotangent.astype(jnp.float32))[0].astype(jnp.bfloat16)
    pulled_group = lax.all_gather(pulled, "team", axis=0, tiled=True)
    partial_back = collect(pulled_group, adj_cols, adj_vals)
    spread = lax.psum_scatter(partial_back, "blk", scatter_dimension=0, tiled=True).astype(
        jnp.bfloat16
    )
    grad_input = jnp.dot(spread, weight.T, preferred_element_type=jnp.float32).astype(jnp.bfloat16)
    local_weight = lax.dot_general(
        features, spread, (((0,), (0,)), ((), ())), preferred_element_type=jnp.float32
    )
    local_bias = jnp.sum(pulled.astype(jnp.float32), axis=0)
    grad_weight, grad_bias = lax.psum((local_weight, local_bias), ("blk", "team"))
    return (hidden, grad_input, grad_weight, grad_bias)


def solution(mesh):
    return jax.shard_map(
        local,
        mesh=mesh,
        in_specs=(
            P(("blk", "team"), None),
            P(),
            P(),
            P(("blk", "team"), None),
            P("team", None, "blk", None),
            P("team", None, "blk", None, None, None),
        ),
        out_specs=(P(("blk", "team"), None), P(("blk", "team"), None), P(), P()),
        check_vma=False,
    )
```

profile of v0, /device:TPU:0, one launch (start us, length us, event | category | flops | bytes accessed | tf_op | source)
XLA Modules:
  0.0 316.7 jit_solution(3122750745222249054)
XLA Ops:
  7.2 0.0 copy-start
  7.2 0.0 all-gather.3.cloned.1.call-start
  7.2 0.7 all-gather.3.cloned.1.call-update
  7.9 0.0 reduce-scatter.3.cloned.1.call-start
  8.0 0.7 compare_select_fusion
  8.6 0.1 reshape.50
  8.7 0.7 compare_and_fusion
  9.4 59.4 %all-gather.3.cloned.1.call-done = bf16[2048,256]{1,0:T(8,128)(2,1)} async-done(((bf16[128,256]{1,0:T(8,128)(2,1)}), bf16[2048,256]{1,0:T(8,128)(2,1)}) %all-gather.3.cloned.1.call-update) | async-done | bytes 1048592 | tf_op jit(solution)/shard_map/all_gather | solution.py:24
  68.8 1.7 convolution_convert_fusion
  70.4 0.6 gather_fusion
  71.1 0.0 copy-done
  71.1 0.0 copy-start.3
  71.1 0.0 copy-start.4
  71.1 1.2 fusion.2
  72.3 0.0 reduce-scatter.3.cloned.1.call-update
  72.4 0.0 all-gather.5.cloned.1.call-start
  72.4 6.6 %reduce-scatter.3.cloned.1.call-done = f32[128,256]{1,0:T(8,128)} async-done(((f32[256,256]{1,0:T(8,128)}), f32[128,256]{1,0:T(8,128)}) %reduce-scatter.3.cloned.1.call-update) | async-done | bytes 131088 | tf_op jit(solution)/shard_map/reduce_scatter | solution.py:29
  79.0 0.0 copy-done.3
  79.0 0.0 copy-done.4
  79.0 1.7 convert_reduce_fusion
  80.7 0.0 all-gather.5.cloned.1.call-update
  80.7 0.0 reduce-scatter.5.cloned.1.call-start
  80.7 58.4 %all-gather.5.cloned.1.call-done = bf16[2048,256]{1,0:T(8,128)(2,1)} async-done(((bf16[128,256]{1,0:T(8,128)(2,1)}), bf16[2048,256]{1,0:T(8,128)(2,1)}) %all-gather.5.cloned.1.call-update) | async-done | bytes 1048592 | tf_op jit(solution)/shard_map/all_gather | solution.py:34
  139.2 1.9 gather_fusion.1
  141.1 0.0 copy-start.2
  141.1 0.0 copy-start.1
  141.1 1.2 fusion
  142.3 0.0 reduce-scatter.5.cloned.1.call-update
  142.3 0.0 all-reduce.2.cloned.1.call-start
  142.4 38.4 %psum.15 = f32[256]{0:T(256)} all-reduce(f32[256]{0:T(256)S(1)} %get-tuple-element.9), channel_id=1, replica_groups=mesh['blk'=2,'team'=16] {'blk','team'}, use_global_device_ids=true, to_apply=%region_4.6 | all-reduce | flops 256 | bytes 2048 | tf_op jit(solution)/shard_map/psum | solution.py:44
  180.8 0.0 reduce-scatter.5.cloned.1.call-done
  180.8 0.0 copy-done.2
  180.8 1.8 convolution_bitcast_fusion
  182.6 0.0 all-reduce.2.cloned.1.call-update
  182.7 0.0 copy-done.1
  182.7 1.7 convolution_convert_fusion.1
  184.4 124.0 %all-reduce.2.cloned.1.call-done = f32[256,256]{0,1:T(8,128)} async-done(((f32[256,256]{0,1:T(8,128)}), f32[256,256]{0,1:T(8,128)}) %all-reduce.2.cloned.1.call-update) | async-done | bytes 262160 | tf_op jit(solution)/shard_map/psum | solution.py:44
  308.4 1.8 copy.10
  (1 shorter events, 0.0 us)
Async XLA Ops:
  7.2 63.9 %copy-start = (bf16[1,2,1,12,128,128]{5,4,3,2,1,0:T(8,128)(2,1)S(1)}, bf16[1,2,1,12,128,128]{5,4,3,2,1,0:T(8,128)(2,1)}, u32[]{:S(2)}) copy-start(bf16[1,2,1,12,128,128]{5,4,3,2,1,0:T(8,128)(2,1)} %param.13) | copy-start | bytes 2359300
  7.2 61.6 %all-gather.3.cloned.1.call-start = ((), (), s32[]{:S(2)}) async-start(), calls=%async_computation.2 | async-start | bytes 1114112 | tf_op jit(solution)/shard_map/all_gather | solution.py:24
  7.9 71.1 %reduce-scatter.3.cloned.1.call-start = ((), (), s32[]{:S(2)}) async-start(), calls=%async_computation.3 | async-start | bytes 393216 | tf_op jit(solution)/shard_map/reduce_scatter | solution.py:29
  71.1 7.9 %copy-start.3 = (bf16[128,256]{1,0:T(8,128)(2,1)S(1)}, bf16[128,256]{1,0:T(8,128)(2,1)}, u32[]{:S(2)}) copy-start(bf16[128,256]{1,0:T(8,128)(2,1)} %param.11) | copy-start | bytes 196612
  71.1 7.9 %copy-start.4 = (f32[256]{0:T(256)S(1)}, f32[256]{0:T(256)}, u32[]{:S(2)}) copy-start(f32[256]{0:T(256)} %param.10) | copy-start | bytes 3076
  72.4 66.8 %all-gather.5.cloned.1.call-start = ((), (), s32[]{:S(2)}) async-start(), calls=%async_computation.4 | async-start | bytes 1114112 | tf_op jit(solution)/shard_map/all_gather | solution.py:34
  80.7 100.1 %reduce-scatter.5.cloned.1.call-start = ((), (), s32[]{:S(2)}) async-start(), calls=%async_computation.5 | async-start | bytes 393216 | tf_op jit(solution)/shard_map/reduce_scatter | solution.py:36
  141.1 39.8 %copy-start.2 = (bf16[128,256]{1,0:T(8,128)(2,1)S(1)}, bf16[128,256]{1,0:T(8,128)(2,1)}, u32[]{:S(2)}) copy-start(bf16[128,256]{1,0:T(8,128)(2,1)} %param.8) | copy-start | bytes 196612
  141.1 41.6 %copy-start.1 = (bf16[256,256]{1,0:T(8,128)(2,1)S(1)}, bf16[256,256]{1,0:T(8,128)(2,1)}, u32[]{:S(2)}) copy-start(bf16[256,256]{1,0:T(8,128)(2,1)} %param.9) | copy-start | bytes 393220
  142.3 166.1 %all-reduce.2.cloned.1.call-start = ((), (), s32[]{:S(2)}) async-start(), calls=%async_computation.6 | async-start | bytes 524288 | tf_op jit(solution)/shard_map/psum | solution.py:44
Sparse Core Ops, SparseCore 0:
  10.8 57.9 all-gather.2
  72.5 6.4 reduce-scatter.2
  82.7 56.4 all-gather.4
  142.4 6.4 reduce-scatter.4
  182.8 125.5 all-reduce.1
where the time goes:
time: 317 us
  waiting for transfers between devices  249 us (79%)
  blocking collectives  38.4 us (12%)
  between operations  13.9 us (4%)
  matrix products  7.62 us (2%)
  local copies, waits for them, and re-layouts  4.42 us (1%)
    psum x1, waiting for transfers between devices, local(): lax.psum((local_weight, local_bias), ('blk', 'team'))  124 us
    all_gather x1, waiting for transfers between devices, local(): lax.all_gather(features, 'team', axis=0, tiled=True)  59.4 us
    all_gather x1, waiting for transfers between devices, local(): pulled_group = lax.all_gather(pulled, 'team', axis=0, tiled=True)  58.4 us
    psum x1, blocking collectives, local(): lax.psum((local_weight, local_bias), ('blk', 'team'))  38.4 us
    reduce_scatter x1, waiting for transfers between devices, local(): lax.psum_scatter(partial_rows, 'blk', scatter_dimension=0, tiled=True)  6.58 us
  transfers between devices with their start and end apart: 5, of which 4 were waited for; matrix products, arithmetic and copies ran while one was open for 1% of the time, Pallas kernels for 0%

commit v1 on v0

v1 whole, which is shorter than its diff:
```python
import functools

import jax
import jax.numpy as jnp
from jax import lax
from jax.experimental import pallas as pl
from jax.experimental.pallas import tpu as pltpu
from jax.sharding import PartitionSpec as P

PLANE = 4
MESH = pl.DeviceIdType.MESH


def flip(index, mask):
    bit = 1
    while bit <= mask:
        if mask & bit:
            index = index + bit - 2 * bit * ((index // bit) % 2)
        bit *= 2
    return index


def kernel(
    blks,
    team,
    rows,
    x_ref,
    w_ref,
    b_ref,
    ct_ref,
    cols_ref,
    vals_ref,
    hidden_ref,
    gi_ref,
    gw_ref,
    gb_ref,
    vals,
    dense,
    xbuf,
    pbuf,
    part,
    ybuf,
    sbuf,
    gpart,
    gl1,
    gtot,
    grs,
    gag,
    vals_sem,
    x_send,
    x_recv,
    p_send,
    p_recv,
    y_send,
    y_recv,
    s_send,
    s_recv,
    l1_send,
    l1_recv,
    rs_send,
    rs_recv,
    ag_send,
    ag_recv,
    l4_send,
    l4_recv,
):
    g = lax.axis_index("blk")
    m = lax.axis_index("team")
    block = x_ref.shape[0]
    width = x_ref.shape[1]
    nnz = vals_ref.shape[3]

    fetch = pltpu.make_async_copy(vals_ref, vals, vals_sem)
    fetch.start()

    barrier = pltpu.get_barrier_semaphore()
    for mask in range(1, team):
        pl.semaphore_signal(
            barrier, inc=1, device_id=(g, flip(m, mask)), device_id_type=MESH
        )
    for mask in range(1, blks):
        pl.semaphore_signal(
            barrier, inc=1, device_id=(flip(g, mask), m), device_id_type=MESH
        )

    def panel(buf, index):
        return buf.at[pl.ds(pl.multiple_of(index * block, block), block)]

    xbuf[pl.ds(pl.multiple_of(m * block, block), block), :] = x_ref[...]
    pl.semaphore_wait(barrier, team + blks - 2)

    pending = []

    def send(src, dst, send_sem, recv_sem, device):
        copy = pltpu.make_async_remote_copy(
            src_ref=src,
            dst_ref=dst,
            send_sem=send_sem,
            recv_sem=recv_sem,
            device_id=device,
            device_id_type=MESH,
        )
        copy.start()
        pending.append(copy)

    def arrived(dst, send_sem, recv_sem):
        pltpu.make_async_remote_copy(
            src_ref=dst,
            dst_ref=dst,
            send_sem=send_sem,
            recv_sem=recv_sem,
            device_id=(g, flip(m, 1)),
            device_id_type=MESH,
        ).wait_recv()

    def gather_open(buf, send_sems, recv_sems):
        own = panel(buf, m)
        for mask in range(PLANE, team, PLANE):
            send(own, own, send_sems.at[mask], recv_sems.at[mask], (g, flip(m, mask)))
        for mask in range(1, PLANE):
            send(own, own, send_sems.at[mask], recv_sems.at[mask], (g, flip(m, mask)))

    def gather_forward(buf, send_sems, recv_sems):
        for far in range(PLANE, team, PLANE):
            item = panel(buf, flip(m, far))
            arrived(item, send_sems.at[far], recv_sems.at[far])
            for near in range(1, PLANE):
                send(
                    item,
                    item,
                    send_sems.at[far + near],
                    recv_sems.at[far + near],
                    (g, flip(m, near)),
                )

    def gather_close(buf, send_sems, recv_sems):
        for far in range(0, team, PLANE):
            for near in range(1, PLANE):
                mask = far + near
                arrived(panel(buf, flip(m, mask)), send_sems.at[mask], recv_sems.at[mask])

    def exchange(src_of, buf, send_sems, recv_sems):
        for mask in range(1, blks):
            peer = flip(g, mask)
            send(src_of(peer), buf.at[g], send_sems.at[mask], recv_sems.at[mask], (peer, m))

    def exchanged(buf, send_sems, recv_sems):
        for mask in range(1, blks):
            arrived(buf.at[flip(g, mask)], send_sems.at[mask], recv_sems.at[mask])

    tall = min(2, blks) * block
    deep = min(8, team) * block

    def aggregate(buf):
        for top in range(0, blks * block, tall):
            if team * block == 2 * deep:
                total = jnp.dot(
                    dense[top : top + tall, :deep],
                    buf[:deep, :],
                    preferred_element_type=jnp.float32,
                )
                part[top : top + tall, :] = total + jnp.dot(
                    dense[top : top + tall, deep:],
                    buf[deep:, :],
                    preferred_element_type=jnp.float32,
                )
            else:
                part[top : top + tall, :] = jnp.zeros((tall, width), jnp.float32)

                def step(i, carry, top=top):
                    span = pl.ds(pl.multiple_of(i * deep, deep), deep)
                    part[top : top + tall, :] += jnp.dot(
                        dense[top : top + tall, span],
                        buf[span, :],
                        preferred_element_type=jnp.float32,
                    )
                    return carry

                lax.fori_loop(0, team * block // deep, step, 0)

    def part_of(peer):
        return panel(part, peer)

    def own_part():
        return part[pl.ds(pl.multiple_of(g * block, block), block), :]

    gather_open(xbuf, x_send, x_recv)
    fetch.wait()

    def lay(c, carry):
        for r in range(blks):
            slot = 0
            found = 0
            for k in range(nnz):
                hit = cols_ref[0, r, 0, k] == c
                slot = jnp.where(hit, k, slot)
                found = jnp.where(hit, 1, found)
            keep = found.astype(jnp.float32)
            item = vals[0, r, 0, slot].astype(jnp.float32) * keep
            span = pl.ds(pl.multiple_of(c * block, block), block)
            dense[r * block : (r + 1) * block, span] = item.astype(jnp.bfloat16)
        return carry

    third = team // PLANE
    lax.fori_loop(0, third, lay, 0)
    gather_forward(xbuf, x_send, x_recv)
    lax.fori_loop(third, team, lay, 0)
    gather_close(xbuf, x_send, x_recv)
    aggregate(xbuf)
    first = len(pending)
    exchange(part_of, ybuf, y_send, y_recv)
    parted = pending[first:]
    del pending[first:]
    y = own_part()
    exchanged(ybuf, y_send, y_recv)
    for mask in range(1, blks):
        y = y + ybuf[flip(g, mask)]
    high = y.astype(jnp.bfloat16)
    low = (y - high.astype(jnp.float32)).astype(jnp.bfloat16)
    weight = w_ref[...]
    pre = (
        jnp.dot(high, weight, preferred_element_type=jnp.float32)
        + jnp.dot(low, weight, preferred_element_type=jnp.float32)
        + b_ref[...]
    )
    square = pre * pre
    bent = jnp.tanh(0.7978845608 * (pre + 0.044715 * (square * pre)))
    half = 0.5 * (1.0 + bent)
    slope = half + (0.5 * pre) * ((1.0 - bent) * (1.0 + bent)) * (
        0.7978845608 * (1.0 + 0.134145 * square)
    )
    pulled = (ct_ref[...].astype(jnp.float32) * slope).astype(jnp.bfloat16)

    pbuf[pl.ds(pl.multiple_of(m * block, block), block), :] = pulled
    gather_open(pbuf, p_send, p_recv)
    hidden_ref[...] = (pre * half).astype(jnp.bfloat16)

    turned = (((0,), (0,)), ((), ()))
    grad = lax.dot_general(high, pulled, turned, preferred_element_type=jnp.float32)
    grad = grad + lax.dot_general(low, pulled, turned, preferred_element_type=jnp.float32)
    count = grad.shape[0] // rows
    chunks = blks * team
    if count < chunks:
        gpart[count:, :, :width] = jnp.zeros((chunks - count, rows, width), jnp.float32)
    gpart[:count, :, :width] = grad.reshape(count, rows, width)
    column = jnp.sum(pulled.astype(jnp.float32), axis=0, keepdims=True)
    lanes = width // 2
    line = lax.broadcasted_iota(jnp.int32, (rows, lanes), 0)
    tail = jnp.where(
        line == 0,
        jnp.broadcast_to(column[:, :lanes], (rows, lanes)),
        jnp.where(line == 1, jnp.broadcast_to(column[:, lanes:], (rows, lanes)), 0.0),
    )
    gpart[:, :, width:] = jnp.broadcast_to(tail[None], (chunks, rows, lanes))
    exchange(lambda peer: gpart.at[pl.ds(peer * team, team)], gl1, l1_send, l1_recv)

    gather_forward(pbuf, p_send, p_recv)

    exchanged(gl1, l1_send, l1_recv)
    total = gpart[pl.ds(g * team, team)]
    for mask in range(1, blks):
        total = total + gl1[flip(g, mask)]
    gtot[...] = total
    for mask in range(1, team):
        peer = flip(m, mask)
        send(gtot.at[peer], grs.at[m], rs_send.at[mask], rs_recv.at[mask], (g, peer))
    grs[m] = gtot[m]
    for mask in range(1, team):
        arrived(grs.at[flip(m, mask)], rs_send.at[mask], rs_recv.at[mask])
    mine = jnp.sum(grs[...], axis=0)
    gag[g, m] = mine[:, :width]
    gb_ref[:, :lanes] = mine[0:1, width:]
    gb_ref[:, lanes:] = mine[1:2, width:]
    for mask in range(1, team):
        send(
            gag.at[g, m],
            gag.at[g, m],
            ag_send.at[mask],
            ag_recv.at[mask],
            (g, flip(m, mask)),
        )

    gather_close(pbuf, p_send, p_recv)
    for copy in parted:
        copy.wait_send()
    aggregate(pbuf)
    exchange(part_of, sbuf, s_send, s_recv)
    for mask in range(1, team):
        arrived(gag.at[g, flip(m, mask)], ag_send.at[mask], ag_recv.at[mask])
    exchange(lambda peer: gag.at[g], gag, l4_send, l4_recv)
    spread = own_part()
    exchanged(sbuf, s_send, s_recv)
    for mask in range(1, blks):
        spread = spread + sbuf[flip(g, mask)]
    gi_ref[...] = lax.dot_general(
        spread.astype(jnp.bfloat16),
        weight,
        (((1,), (1,)), ((), ())),
        preferred_element_type=jnp.float32,
    ).astype(jnp.bfloat16)
    exchanged(gag, l4_send, l4_recv)
    gw_ref[...] = gag[...].reshape(chunks * rows, width)[: gw_ref.shape[0]]
    for copy in pending:
        copy.wait_send()


def local(blks, team, features, weight, bias, cotangent, adj_cols, adj_vals):
    block, width = features.shape
    rows = 8 * pl.cdiv(width, 8 * blks * team)
    wide = width + width // 2
    f32, bf16 = jnp.float32, jnp.bfloat16
    dma = pltpu.SemaphoreType.DMA
    vmem = pl.BlockSpec(memory_space=pltpu.VMEM)
    panels = blks * block
    hidden, grad_input, grad_weight, grad_bias = pl.pallas_call(
        functools.partial(kernel, blks, team, rows),
        out_shape=(
            jax.ShapeDtypeStruct((block, width), bf16),
            jax.ShapeDtypeStruct((block, width), bf16),
            jax.ShapeDtypeStruct((width, width), f32),
            jax.ShapeDtypeStruct((1, width), f32),
        ),
        in_specs=[
            vmem,
            vmem,
            vmem,
            vmem,
            pl.BlockSpec(memory_space=pltpu.SMEM),
            pl.BlockSpec(memory_space=pl.ANY),
        ],
        out_specs=(vmem, vmem, vmem, vmem),
        scratch_shapes=[
            pltpu.VMEM(adj_vals.shape, bf16),
            pltpu.VMEM((panels, team * block), bf16),
            pltpu.VMEM((team * block, width), bf16),
            pltpu.VMEM((team * block, width), bf16),
            pltpu.VMEM((panels, width), f32),
            pltpu.VMEM((blks, block, width), f32),
            pltpu.VMEM((blks, block, width), f32),
            pltpu.VMEM((blks * team, rows, wide), f32),
            pltpu.VMEM((blks, team, rows, wide), f32),
            pltpu.VMEM((team, rows, wide), f32),
            pltpu.VMEM((team, rows, wide), f32),
            pltpu.VMEM((blks, team, rows, width), f32),
            dma,
            dma((team,)),
            dma((team,)),
            dma((team,)),
            dma((team,)),
            dma((blks,)),
            dma((blks,)),
            dma((blks,)),
            dma((blks,)),
            dma((blks,)),
            dma((blks,)),
            dma((team,)),
            dma((team,)),
            dma((team,)),
            dma((team,)),
            dma((blks,)),
            dma((blks,)),
        ],
        compiler_params=pltpu.CompilerParams(
            collective_id=0, has_side_effects=True, vmem_limit_bytes=56 * 2**20
        ),
    )(features, weight, bias.reshape(1, width), cotangent, adj_cols, adj_vals)
    return hidden, grad_input, grad_weight, grad_bias.reshape(width)


def solution(mesh):
    return jax.shard_map(
        functools.partial(local, mesh.shape["blk"], mesh.shape["team"]),
        mesh=mesh,
        in_specs=(
            P(("blk", "team"), None),
            P(),
            P(),
            P(("blk", "team"), None),
            P("team", None, "blk", None),
            P("team", None, "blk", None, None, None),
        ),
        out_specs=(P(("blk", "team"), None), P(("blk", "team"), None), P(), P()),
        check_vma=False,
    )
```

time: 317 us -> 51.7 us (0.16)
  waiting for transfers between devices: 249 us -> 0 us
  Pallas kernels: 0 us -> 46.6 us
  blocking collectives: 38.4 us -> 0 us
  between operations: 13.9 us -> 0.65 us
  matrix products: 7.62 us -> 0 us
    psum x1 -> x0, waiting for transfers between devices: 124 us -> none  [local(): lax.psum((local_weight, local_bias), ('blk', 'team'))]
    all_gather x2 -> x0, waiting for transfers between devices: 118 us -> none  [the longest x1 59.4 us: local(): lax.all_gather(features, 'team', axis=0, tiled=True)]
    pallas_call x0 -> x1, Pallas kernels: none -> 46.6 us  [local(): pl.pallas_call(functools.partial(kernel, blks, team, rows), out_shape=(ja...]
    psum x1 -> x0, blocking collectives: 38.4 us -> none  [local(): lax.psum((local_weight, local_bias), ('blk', 'team'))]
    dot_general x5 -> x0, matrix products: 7.62 us -> none  [the longest x2 2.41 us: collect(): jnp.einsum('rkij,rkjf->rif', adj_vals[0, :, 0], picked, preferred_element...]
    reduce_scatter x2 -> x0, waiting for transfers between devices: 6.58 us -> none  [the longest x1 6.58 us: local(): lax.psum_scatter(partial_rows, 'blk', scatter_dimension=0, tiled=True)]
  transfers between devices with their start and end apart: 5 -> 0, of which waited for: 4 -> 0; matrix products, arithmetic and copies ran while one was open for 1% -> 0% of each run, Pallas kernels for 0% -> 0%
where the time goes in v1:
time: 51.7 us; the launch traced here: 51.5 us
  Pallas kernels  46.6 us (90%)
  local copies, waits for them, and re-layouts  4.26 us (8%)
  between operations  0.65 us (1%)
    pallas_call x1, Pallas kernels, local(): pl.pallas_call(functools.partial(kernel, blks, team, rows), out_shape=(ja...  46.6 us
    unnamed x8, local copies, waits for them, and re-layouts  4.26 us

profile of v1, /device:TPU:0, one launch (start us, length us, event | category | flops | bytes accessed | tf_op | source)
XLA Modules:
  0.0 51.5 jit_solution(10170406605388635404)
XLA Ops:
  0.6 46.6 %shard_map.93 = (bf16[128,256]{1,0:T(8,128)(2,1)}, bf16[128,256]{1,0:T(8,128)(2,1)}, f32[256,256]{1,0:T(8,128)}, f32[1,256]{1,0:T(1,128)}) custom-call(bf16[128,256]{1,0:T(8,128)(2,1)} %x_ref.1, bf16[256,256]{1,0:T(8,128)(2,1)} %w_ref.1, f32[1,256]{1,0:T(1,128)} %bitcast.3, bf16[128,256]{1,0:T(8,128)(2,1)} %ct_ref.1, s32[1,2,1,12]{3,2,1,0:T(1,128)} %cols_ref.1, ...), custom_call_target="tpu_custom_call" | custom-call | tf_op jit(solution)/shard_map/pallas_call | solution.py:315
  47.2 0.0 copy-start
  47.2 1.5 %copy.14 = bf16[128,256]{1,0:T(8,128)(2,1)} copy(bf16[128,256]{1,0:T(8,128)(2,1)} %get-tuple-element.16) | data formatting | bytes 131072
  48.7 1.5 %copy.15 = bf16[128,256]{1,0:T(8,128)(2,1)} copy(bf16[128,256]{1,0:T(8,128)(2,1)} %get-tuple-element.17) | data formatting | bytes 131072
  50.2 0.0 copy-done
  50.2 0.0 copy-start.1
  50.2 0.7 %copy.16 = f32[256,256]{1,0:T(8,128)} copy(f32[256,256]{1,0:T(8,128)S(1)} %copy-done) | data formatting | bytes 524288
  50.9 0.0 copy-done.1
  50.9 0.6 %copy.17 = f32[256]{0:T(256)} copy(f32[256]{0:T(256)S(1)} %bitcast.2) | data formatting | bytes 2048
Async XLA Ops:
  47.2 3.0 %copy-start = (f32[256,256]{1,0:T(8,128)S(1)}, f32[256,256]{1,0:T(8,128)}, u32[]{:S(2)}) copy-start(f32[256,256]{1,0:T(8,128)} %get-tuple-element.18) | copy-start | bytes 786436
  50.2 0.7 %copy-start.1 = (f32[1,256]{1,0:T(1,128)S(1)}, f32[1,256]{1,0:T(1,128)}, u32[]{:S(2)}) copy-start(f32[1,256]{1,0:T(1,128)} %get-tuple-element.11) | copy-start | bytes 3076

commit v2 on v0

v2 whole, which is shorter than its diff:
```python
import functools
import math

import jax
import jax.numpy as jnp
from jax import lax
from jax.experimental import pallas as pl
from jax.experimental.pallas import tpu as pltpu
from jax.sharding import PartitionSpec as P

PLANE = 4
MESH = pl.DeviceIdType.MESH


def flip(index, mask):
    bit = 1
    while bit <= mask:
        if mask & bit:
            index = index + bit - 2 * bit * ((index // bit) % 2)
        bit *= 2
    return index


def kernel(
    blks,
    team,
    x_ref,
    w_ref,
    b_ref,
    ct_ref,
    cols_ref,
    vals_ref,
    hidden_ref,
    gi_ref,
    gw_ref,
    gb_ref,
    vals,
    dense,
    xbuf,
    pbuf,
    part,
    back,
    ybuf,
    sbuf,
    gpart,
    gl1,
    gtot,
    gplane,
    gsum,
    gline,
    gag,
    vals_sem,
    x_send,
    x_recv,
    x_send2,
    x_recv2,
    p_send,
    p_recv,
    p_send2,
    p_recv2,
    y_send,
    y_recv,
    s_send,
    s_recv,
    l1_send,
    l1_recv,
    rs_send,
    rs_recv,
    ag_send,
    ag_recv,
    l4_send,
    l4_recv,
):
    g = lax.axis_index("blk")
    m = lax.axis_index("team")
    block = x_ref.shape[0]
    width = x_ref.shape[1]
    nnz = vals_ref.shape[3]
    line = team // PLANE
    z, p = m // PLANE, m % PLANE
    half = block // 2
    fars = list(range(PLANE, team, PLANE))

    fetch = pltpu.make_async_copy(vals_ref, vals, vals_sem)
    fetch.start()

    barrier = pltpu.get_barrier_semaphore()
    partners = list(range(1, PLANE)) + fars
    for mask in partners:
        pl.semaphore_signal(
            barrier, inc=1, device_id=(g, flip(m, mask)), device_id_type=MESH
        )
    for mask in range(1, blks):
        pl.semaphore_signal(
            barrier, inc=1, device_id=(flip(g, mask), m), device_id_type=MESH
        )

    def rows_of(index, start=0, size=block):
        return pl.ds(pl.multiple_of(index * block + start, half), size)

    xbuf[rows_of(m), :] = x_ref[...]
    fetch.wait()

    def lay(c, carry):
        for r in range(blks):
            slot = 0
            found = 0
            for k in range(nnz):
                hit = cols_ref[0, r, 0, k] == c
                slot = jnp.where(hit, k, slot)
                found = jnp.where(hit, 1, found)
            keep = found.astype(jnp.float32)
            item = vals[0, r, 0, slot].astype(jnp.float32) * keep
            span = pl.ds(pl.multiple_of(c * block, block), block)
            dense[r * block : (r + 1) * block, span] = item.astype(jnp.bfloat16)
        return carry

    lax.fori_loop(0, team // 4, lay, 0)
    dense[blks * block :, :] = jnp.ones((16, team * block), jnp.bfloat16)
    pl.semaphore_wait(barrier, len(partners) + blks - 1)

    pending = []

    def send(src, dst, send_sem, recv_sem, device):
        copy = pltpu.make_async_remote_copy(
            src_ref=src,
            dst_ref=dst,
            send_sem=send_sem,
            recv_sem=recv_sem,
            device_id=device,
            device_id_type=MESH,
        )
        copy.start()
        pending.append(copy)

    def arrived(dst, send_sem, recv_sem):
        pltpu.make_async_remote_copy(
            src_ref=dst,
            dst_ref=dst,
            send_sem=send_sem,
            recv_sem=recv_sem,
            device_id=(g, flip(m, 1)),
            device_id_type=MESH,
        ).wait_recv()

    class Gather:
        def __init__(self, buf, sends, recvs, sends2, recvs2):
            self.buf = buf
            self.sems = (sends, recvs)
            self.sems2 = (sends2, recvs2)

        def item(self, mask):
            return self.buf.at[rows_of(flip(m, mask))]

        def spread(self, far):
            for near in (1, 2):
                item = self.item(far)
                sends, recvs = self.sems
                send(item, item, sends.at[far + near], recvs.at[far + near], (g, flip(m, near)))

        def open(self):
            self.spread(0)
            sends, recvs = self.sems
            for far in fars:
                item = self.item(0)
                send(item, item, sends.at[far], recvs.at[far], (g, flip(m, far)))

        def wait(self, mask):
            sends, recvs = self.sems
            arrived(self.item(mask), sends.at[mask], recvs.at[mask])

        def forward(self, far):
            self.wait(far)
            self.spread(far)

        def cross(self, far):
            for near, sems, start in ((1, self.sems, 0), (2, self.sems2, half)):
                self.wait(far + near)
                item = self.buf.at[rows_of(flip(m, far + near), start, half)]
                mask = far + 3
                send(item, item, sems[0].at[mask], sems[1].at[mask], (g, flip(m, 3 - near)))

        def close(self):
            for far in [0] + fars:
                mask = far + 3
                for sems, start in ((self.sems, 0), (self.sems2, half)):
                    item = self.buf.at[rows_of(flip(m, mask), start, half)]
                    arrived(item, sems[0].at[mask], sems[1].at[mask])

    def exchange(src_of, buf, send_sems, recv_sems):
        for mask in range(1, blks):
            peer = flip(g, mask)
            send(src_of(peer), buf.at[g], send_sems.at[mask], recv_sems.at[mask], (peer, m))

    def exchanged(buf, send_sems, recv_sems):
        for mask in range(1, blks):
            arrived(buf.at[flip(g, mask)], send_sems.at[mask], recv_sems.at[mask])

    deep = min(8, team) * block

    def aggregate(buf, top, tall):
        def term(span):
            return jnp.dot(
                dense[top : top + tall, span],
                buf[span, :],
                preferred_element_type=jnp.float32,
            )

        if team * block <= 2 * deep:
            return sum(term(slice(i, i + deep)) for i in range(0, team * block, deep))

        def step(i, total):
            return total + term(pl.ds(pl.multiple_of(i * deep, deep), deep))

        start = jnp.zeros((tall, width), jnp.float32)
        return lax.fori_loop(0, team * block // deep, step, start)

    tall = min(2, blks) * block

    xs = Gather(xbuf, x_send, x_recv, x_send2, x_recv2)
    xs.open()
    lax.fori_loop(team // 4, team // 2, lay, 0)
    for place, far in enumerate(fars):
        xs.forward(far)
        xs.cross(far - PLANE)
    lax.fori_loop(team // 2, team, lay, 0)
    xs.cross(fars[-1])
    xs.close()
    for top in range(0, blks * block, tall):
        part[pl.ds(top // block, tall // block)] = aggregate(xbuf, top, tall).reshape(
            tall // block, block, width
        )
    exchange(lambda peer: part.at[peer], ybuf, y_send, y_recv)
    y = part[g]
    exchanged(ybuf, y_send, y_recv)
    for mask in range(1, blks):
        y = y + ybuf[flip(g, mask)]
    high = y.astype(jnp.bfloat16)
    low = (y - high.astype(jnp.float32)).astype(jnp.bfloat16)
    weight = w_ref[...]
    pre = (
        jnp.dot(high, weight, preferred_element_type=jnp.float32)
        + jnp.dot(low, weight, preferred_element_type=jnp.float32)
        + b_ref[...]
    )
    square = pre * pre
    bent = jnp.tanh(0.7978845608 * (pre + 0.044715 * (square * pre)))
    gate = 0.5 * (1.0 + bent)
    slope = gate + (0.5 * pre) * ((1.0 - bent) * (1.0 + bent)) * (
        0.7978845608 * (1.0 + 0.134145 * square)
    )
    pulled = (ct_ref[...].astype(jnp.float32) * slope).astype(jnp.bfloat16)

    pbuf[rows_of(m), :] = pulled
    ps = Gather(pbuf, p_send, p_recv, p_send2, p_recv2)
    ps.open()
    turned = (((0,), (0,)), ((), ()))
    grad = lax.dot_general(high, pulled, turned, preferred_element_type=jnp.float32)
    grad = grad + lax.dot_general(low, pulled, turned, preferred_element_type=jnp.float32)
    chunk = gpart.shape[3]
    count = width // chunk
    chunks = blks * team
    whole = grad.reshape(count, chunk, width)
    if count < chunks:
        empty = jnp.zeros((chunks - count, chunk, width), jnp.float32)
        whole = jnp.concatenate([whole, empty], axis=0)
    gpart[...] = whole.reshape(blks, PLANE, line, chunk, width)
    exchange(lambda peer: gpart.at[peer], gl1, l1_send, l1_recv)
    hidden_ref[...] = (pre * gate).astype(jnp.bfloat16)

    ps.forward(fars[0])
    ps.cross(0)

    exchanged(gl1, l1_send, l1_recv)
    total = gpart[g]
    for mask in range(1, blks):
        total = total + gl1[flip(g, mask)]
    gtot[...] = total
    for near in range(1, PLANE):
        send(
            gtot.at[flip(p, near)],
            gplane.at[p],
            rs_send.at[near],
            rs_recv.at[near],
            (g, flip(m, near)),
        )
    gplane[p] = gtot[p]

    for far in fars[1:]:
        ps.forward(far)
        ps.cross(far - PLANE)
    for near in range(1, PLANE):
        arrived(gplane.at[flip(p, near)], rs_send.at[near], rs_recv.at[near])
    gsum[...] = jnp.sum(gplane[...], axis=0)
    for far in fars:
        send(
            gsum.at[flip(z, far // PLANE)],
            gline.at[z],
            rs_send.at[far],
            rs_recv.at[far],
            (g, flip(m, far)),
        )
    gline[z] = gsum[z]
    ps.cross(fars[-1])
    for far in fars:
        arrived(gline.at[flip(z, far // PLANE)], rs_send.at[far], rs_recv.at[far])
    gag[g, z, p] = jnp.sum(gline[...], axis=0)
    for near in range(1, PLANE):
        item = gag.at[g, z, p]
        send(item, item, ag_send.at[near], ag_recv.at[near], (g, flip(m, near)))
    ps.close()
    for top in range(0, blks * block, tall):
        extra = 16 if top + tall == blks * block else 0
        total = aggregate(pbuf, top, tall + extra)
        back[pl.ds(top // block, tall // block), :block] = total[:tall].reshape(
            tall // block, block, width
        )
    for r in range(blks):
        back[r, block:] = total[tall : tall + 8]
    exchange(lambda peer: back.at[peer], sbuf, s_send, s_recv)
    for near in range(1, PLANE):
        arrived(gag.at[g, z, flip(p, near)], ag_send.at[near], ag_recv.at[near])
    for far in fars:
        item = gag.at[g, z]
        send(item, item, ag_send.at[far], ag_recv.at[far], (g, flip(m, far)))
    spread = back[g]
    exchanged(sbuf, s_send, s_recv)
    for mask in range(1, blks):
        spread = spread + sbuf[flip(g, mask)]
    gi_ref[...] = lax.dot_general(
        spread[:block].astype(jnp.bfloat16),
        weight,
        (((1,), (1,)), ((), ())),
        preferred_element_type=jnp.float32,
    ).astype(jnp.bfloat16)
    gb_ref[...] = spread[block : block + 1]
    for far in fars:
        arrived(gag.at[g, flip(z, far // PLANE)], ag_send.at[far], ag_recv.at[far])
    exchange(lambda peer: gag.at[g], gag, l4_send, l4_recv)
    exchanged(gag, l4_send, l4_recv)
    for i in range(count):
        b, q, l = i // team, i // line % PLANE, i % line
        gw_ref[i * chunk : (i + 1) * chunk] = gag[b, l, q]
    for copy in pending:
        copy.wait_send()


def hand_out(*refs):
    count = len(refs) // 2
    sems = refs[-1]
    copies = [
        pltpu.make_async_copy(refs[i], refs[count + i], sems.at[i]) for i in range(count)
    ]
    for copy in copies:
        copy.start()
    for copy in copies:
        copy.wait()


def local(blks, team, features, weight, bias, cotangent, adj_cols, adj_vals):
    block, width = features.shape
    line = team // PLANE
    chunk = 8 * pl.cdiv(width, 8 * blks * team)
    f32, bf16 = jnp.float32, jnp.bfloat16
    dma = pltpu.SemaphoreType.DMA
    vmem = pl.BlockSpec(memory_space=pltpu.VMEM)
    anywhere = pl.BlockSpec(memory_space=pl.ANY)
    panels = blks * block
    outs = (
        jax.ShapeDtypeStruct((block, width), bf16),
        jax.ShapeDtypeStruct((block, width), bf16),
        jax.ShapeDtypeStruct((width, width), f32),
        jax.ShapeDtypeStruct((1, width), f32),
    )
    buffers = [
        (adj_vals.shape, bf16),
        ((panels + 16, team * block), bf16),
        ((team * block, width), bf16),
        ((team * block, width), bf16),
        ((blks, block, width), f32),
        ((blks, block + 8, width), f32),
        ((blks, block, width), f32),
        ((blks, block + 8, width), f32),
        ((blks, PLANE, line, chunk, width), f32),
        ((blks, PLANE, line, chunk, width), f32),
        ((PLANE, line, chunk, width), f32),
        ((PLANE, line, chunk, width), f32),
        ((line, chunk, width), f32),
        ((line, chunk, width), f32),
        ((blks, line, PLANE, chunk, width), f32),
    ]
    held = sum(math.prod(shape) * jnp.dtype(kind).itemsize for shape, kind in buffers)
    results = pl.pallas_call(
        functools.partial(kernel, blks, team),
        out_shape=outs,
        in_specs=[vmem, vmem, vmem, vmem, pl.BlockSpec(memory_space=pltpu.SMEM), anywhere],
        out_specs=(vmem,) * 4,
        scratch_shapes=[pltpu.VMEM(shape, kind) for shape, kind in buffers]
        + [dma]
        + [dma((team,))] * 8
        + [dma((blks,))] * 6
        + [dma((team,))] * 4
        + [dma((blks,))] * 2,
        compiler_params=pltpu.CompilerParams(
            collective_id=0, has_side_effects=True, vmem_limit_bytes=held + 12 * 2**20
        ),
    )(features, weight, bias.reshape(1, width), cotangent, adj_cols, adj_vals)
    hidden, grad_input, grad_weight, grad_bias = pl.pallas_call(
        hand_out,
        out_shape=outs,
        in_specs=[anywhere] * 4,
        out_specs=(anywhere,) * 4,
        scratch_shapes=[dma((4,))],
    )(*results)
    return hidden, grad_input, grad_weight, grad_bias.reshape(width)


def solution(mesh):
    return jax.shard_map(
        functools.partial(local, mesh.shape["blk"], mesh.shape["team"]),
        mesh=mesh,
        in_specs=(
            P(("blk", "team"), None),
            P(),
            P(),
            P(("blk", "team"), None),
            P("team", None, "blk", None),
            P("team", None, "blk", None, None, None),
        ),
        out_specs=(P(("blk", "team"), None), P(("blk", "team"), None), P(), P()),
        check_vma=False,
    )
```

time: 317 us -> 70.5 us (0.22)
  waiting for transfers between devices: 249 us -> 0 us
  Pallas kernels: 0 us -> 61.9 us
  blocking collectives: 38.4 us -> 0 us
  between operations: 13.9 us -> 0.67 us
  matrix products: 7.62 us -> 0 us
    psum x1 -> x0, waiting for transfers between devices: 124 us -> none  [local(): lax.psum((local_weight, local_bias), ('blk', 'team'))]
    all_gather x2 -> x0, waiting for transfers between devices: 118 us -> none  [the longest x1 59.4 us: local(): lax.all_gather(features, 'team', axis=0, tiled=True)]
    pallas_call x0 -> x2, Pallas kernels: none -> 61.9 us  [the longest x1 48.9 us: local(): pl.pallas_call(functools.partial(kernel, blks, team), out_shape=outs, in_...]
    psum x1 -> x0, blocking collectives: 38.4 us -> none  [local(): lax.psum((local_weight, local_bias), ('blk', 'team'))]
    dot_general x5 -> x0, matrix products: 7.62 us -> none  [the longest x2 2.41 us: collect(): jnp.einsum('rkij,rkjf->rif', adj_vals[0, :, 0], picked, preferred_element...]
    reduce_scatter x2 -> x0, waiting for transfers between devices: 6.58 us -> none  [the longest x1 6.58 us: local(): lax.psum_scatter(partial_rows, 'blk', scatter_dimension=0, tiled=True)]
    unnamed x11 -> x20, local copies, waits for them, and re-layouts: 1.82 us -> 7.58 us
  transfers between devices with their start and end apart: 5 -> 0, of which waited for: 4 -> 0; matrix products, arithmetic and copies ran while one was open for 1% -> 0% of each run, Pallas kernels for 0% -> 0%
where the time goes in v2:
time: 70.5 us; the launch traced here: 70.2 us
  Pallas kernels  61.9 us (88%)
  local copies, waits for them, and re-layouts  7.58 us (11%)
    pallas_call x1, Pallas kernels, local(): pl.pallas_call(functools.partial(kernel, blks, team), out_shape=outs, in_...  48.9 us
    pallas_call x1, Pallas kernels, local(): pl.pallas_call(hand_out, out_shape=outs, in_specs=[anywhere] * 4, out_spe...  13.1 us
    unnamed x20, local copies, waits for them, and re-layouts  7.58 us

profile of v2, /device:TPU:0, one launch (start us, length us, event | category | flops | bytes accessed | tf_op | source)
XLA Modules:
  0.0 70.2 jit_solution(11780480292402150584)
XLA Ops:
  0.6 0.0 copy-start.8
  0.6 0.7 copy-done.8
  1.3 0.0 copy-start
  1.3 1.1 %copy-done = bf16[1,2,1,12,128,128]{5,4,3,2,1,0:T(8,128)(2,1)S(1)} copy-done((bf16[1,2,1,12,128,128]{5,4,3,2,1,0:T(8,128)(2,1)S(1)}, bf16[1,2,1,12,128,128]{5,4,3,2,1,0:T(8,128)(2,1)}, u32[]{:S(2)}) %copy-start) | copy-done | bytes 786456
  2.4 0.0 copy-start.2
  2.4 0.9 %copy-done.2 = bf16[256,256]{1,0:T(8,128)(2,1)S(1)} copy-done((bf16[256,256]{1,0:T(8,128)(2,1)S(1)}, bf16[256,256]{1,0:T(8,128)(2,1)}, u32[]{:S(2)}) %copy-start.2) | copy-done | bytes 131096
  3.4 0.0 copy-start.3
  3.4 0.8 %copy-done.3 = bf16[128,256]{1,0:T(8,128)(2,1)S(1)} copy-done((bf16[128,256]{1,0:T(8,128)(2,1)S(1)}, bf16[128,256]{1,0:T(8,128)(2,1)}, u32[]{:S(2)}) %copy-start.3) | copy-done | bytes 65560
  4.2 0.0 copy-start.4
  4.2 0.8 %copy-done.4 = bf16[128,256]{1,0:T(8,128)(2,1)S(1)} copy-done((bf16[128,256]{1,0:T(8,128)(2,1)S(1)}, bf16[128,256]{1,0:T(8,128)(2,1)}, u32[]{:S(2)}) %copy-start.4) | copy-done | bytes 65560
  5.0 0.0 copy-start.9
  5.0 0.7 copy-done.9
  5.7 48.9 %shard_map.93 = (bf16[128,256]{1,0:T(8,128)(2,1)S(1)}, bf16[128,256]{1,0:T(8,128)(2,1)S(1)}, f32[256,256]{1,0:T(8,128)S(1)}, f32[1,256]{1,0:T(1,128)S(1)}) custom-call(bf16[128,256]{1,0:T(8,128)(2,1)S(1)} %copy-done.3, bf16[256,256]{1,0:T(8,128)(2,1)S(1)} %copy-done.2, f32[1,256]{1,0:T(1,128)S(1)} %bitcast.2, bf16[128,256]{1,0:T(8,128)(2,1)S(1)} %copy-done.4, ...), custom_call_target="tpu_custom_call" | custom-call | tf_op jit(solution)/shard_map/pallas_call | solution.py:393
  54.6 0.0 copy-start.1
  54.6 0.7 copy-done.1
  55.3 0.0 copy-start.5
  55.3 0.6 copy-done.5
  55.9 0.0 copy-start.6
  55.9 0.6 copy-done.6
  56.5 0.0 copy-start.7
  56.5 0.6 copy-done.7
  57.1 13.1 %shard_map.94 = (bf16[128,256]{1,0:T(8,128)(2,1)}, bf16[128,256]{1,0:T(8,128)(2,1)}, f32[256,256]{1,0:T(8,128)}, f32[1,256]{1,0:T(1,128)}) custom-call(bf16[128,256]{1,0:T(8,128)(2,1)} %copy-done.5, bf16[128,256]{1,0:T(8,128)(2,1)} %copy-done.6, f32[256,256]{1,0:T(8,128)} %copy-done.1, f32[1,256]{1,0:T(1,128)} %copy-done.7), custom_call_target="tpu_custom_call" | custom-call | tf_op jit(solution)/shard_map/pallas_call | solution.py:408
Async XLA Ops:
  0.6 0.7 copy-start.8
  1.3 1.1 %copy-start = (bf16[1,2,1,12,128,128]{5,4,3,2,1,0:T(8,128)(2,1)S(1)}, bf16[1,2,1,12,128,128]{5,4,3,2,1,0:T(8,128)(2,1)}, u32[]{:S(2)}) copy-start(bf16[1,2,1,12,128,128]{5,4,3,2,1,0:T(8,128)(2,1)} %vals_ref.1) | copy-start | bytes 2359300
  2.4 0.9 %copy-start.2 = (bf16[256,256]{1,0:T(8,128)(2,1)S(1)}, bf16[256,256]{1,0:T(8,128)(2,1)}, u32[]{:S(2)}) copy-start(bf16[256,256]{1,0:T(8,128)(2,1)} %w_ref.1) | copy-start | bytes 393220
  3.4 0.8 %copy-start.3 = (bf16[128,256]{1,0:T(8,128)(2,1)S(1)}, bf16[128,256]{1,0:T(8,128)(2,1)}, u32[]{:S(2)}) copy-start(bf16[128,256]{1,0:T(8,128)(2,1)} %x_ref.1) | copy-start | bytes 196612
  4.2 0.8 %copy-start.4 = (bf16[128,256]{1,0:T(8,128)(2,1)S(1)}, bf16[128,256]{1,0:T(8,128)(2,1)}, u32[]{:S(2)}) copy-start(bf16[128,256]{1,0:T(8,128)(2,1)} %ct_ref.1) | copy-start | bytes 196612
  5.0 0.7 copy-start.9
  54.6 0.7 %copy-start.1 = (f32[256,256]{1,0:T(8,128)}, f32[256,256]{1,0:T(8,128)S(1)}, u32[]{:S(2)}) copy-start(f32[256,256]{1,0:T(8,128)S(1)} %get-tuple-element.14.refs_2_) | copy-start | bytes 786436
  55.3 0.6 copy-start.5
  55.9 0.6 copy-start.6
  56.5 0.6 copy-start.7

commit v3 on v2

--- a/solution.py
+++ b/solution.py
@@ -1,5 +1,4 @@
 import functools
-import math
 
 import jax
 import jax.numpy as jnp
@@ -45,9 +44,7 @@
     gpart,
     gl1,
     gtot,
-    gplane,
-    gsum,
-    gline,
+    grs,
     gag,
     vals_sem,
     x_send,
@@ -76,8 +73,6 @@
     block = x_ref.shape[0]
     width = x_ref.shape[1]
     nnz = vals_ref.shape[3]
-    line = team // PLANE
-    z, p = m // PLANE, m % PLANE
     half = block // 2
     fars = list(range(PLANE, team, PLANE))
 
@@ -257,57 +252,39 @@
     turned = (((0,), (0,)), ((), ()))
     grad = lax.dot_general(high, pulled, turned, preferred_element_type=jnp.float32)
     grad = grad + lax.dot_general(low, pulled, turned, preferred_element_type=jnp.float32)
-    chunk = gpart.shape[3]
+    chunk = gpart.shape[2]
     count = width // chunk
     chunks = blks * team
     whole = grad.reshape(count, chunk, width)
     if count < chunks:
         empty = jnp.zeros((chunks - count, chunk, width), jnp.float32)
         whole = jnp.concatenate([whole, empty], axis=0)
-    gpart[...] = whole.reshape(blks, PLANE, line, chunk, width)
+    gpart[...] = whole.reshape(blks, team, chunk, width)
     exchange(lambda peer: gpart.at[peer], gl1, l1_send, l1_recv)
-    hidden_ref[...] = (pre * gate).astype(jnp.bfloat16)
-
     ps.forward(fars[0])
-    ps.cross(0)
 
     exchanged(gl1, l1_send, l1_recv)
     total = gpart[g]
     for mask in range(1, blks):
         total = total + gl1[flip(g, mask)]
     gtot[...] = total
-    for near in range(1, PLANE):
-        send(
-            gtot.at[flip(p, near)],
-            gplane.at[p],
-            rs_send.at[near],
-            rs_recv.at[near],
-            (g, flip(m, near)),
-        )
-    gplane[p] = gtot[p]
-
+    for mask in range(1, team):
+        peer = flip(m, mask)
+        send(gtot.at[peer], grs.at[m], rs_send.at[mask], rs_recv.at[mask], (g, peer))
+    grs[m] = gtot[m]
+    hidden_ref[...] = (pre * gate).astype(jnp.bfloat16)
+
+    ps.cross(0)
     for far in fars[1:]:
         ps.forward(far)
         ps.cross(far - PLANE)
-    for near in range(1, PLANE):
-        arrived(gplane.at[flip(p, near)], rs_send.at[near], rs_recv.at[near])
-    gsum[...] = jnp.sum(gplane[...], axis=0)
-    for far in fars:
-        send(
-            gsum.at[flip(z, far // PLANE)],
-            gline.at[z],
-            rs_send.at[far],
-            rs_recv.at[far],
-            (g, flip(m, far)),
-        )
-    gline[z] = gsum[z]
+    for mask in range(1, team):
+        arrived(grs.at[flip(m, mask)], rs_send.at[mask], rs_recv.at[mask])
+    gag[g, m] = jnp.sum(grs[...], axis=0)
+    for mask in range(1, team):
+        item = gag.at[g, m]
+        send(item, item, ag_send.at[mask], ag_recv.at[mask], (g, flip(m, mask)))
     ps.cross(fars[-1])
-    for far in fars:
-        arrived(gline.at[flip(z, far // PLANE)], rs_send.at[far], rs_recv.at[far])
-    gag[g, z, p] = jnp.sum(gline[...], axis=0)
-    for near in range(1, PLANE):
-        item = gag.at[g, z, p]
-        send(item, item, ag_send.at[near], ag_recv.at[near], (g, flip(m, near)))
     ps.close()
     for top in range(0, blks * block, tall):
         extra = 16 if top + tall == blks * block else 0
@@ -318,11 +295,9 @@
     for r in range(blks):
         back[r, block:] = total[tall : tall + 8]
     exchange(lambda peer: back.at[peer], sbuf, s_send, s_recv)
-    for near in range(1, PLANE):
-        arrived(gag.at[g, z, flip(p, near)], ag_send.at[near], ag_recv.at[near])
-    for far in fars:
-        item = gag.at[g, z]
-        send(item, item, ag_send.at[far], ag_recv.at[far], (g, flip(m, far)))
+    for mask in range(1, team):
+        arrived(gag.at[g, flip(m, mask)], ag_send.at[mask], ag_recv.at[mask])
+    exchange(lambda peer: gag.at[g], gag, l4_send, l4_recv)
     spread = back[g]
     exchanged(sbuf, s_send, s_recv)
     for mask in range(1, blks):
@@ -334,32 +309,33 @@
         preferred_element_type=jnp.float32,
     ).astype(jnp.bfloat16)
     gb_ref[...] = spread[block : block + 1]
-    for far in fars:
-        arrived(gag.at[g, flip(z, far // PLANE)], ag_send.at[far], ag_recv.at[far])
-    exchange(lambda peer: gag.at[g], gag, l4_send, l4_recv)
     exchanged(gag, l4_send, l4_recv)
-    for i in range(count):
-        b, q, l = i // team, i // line % PLANE, i % line
-        gw_ref[i * chunk : (i + 1) * chunk] = gag[b, l, q]
+    gw_ref[...] = gag[...].reshape(chunks * chunk, width)[:width]
     for copy in pending:
         copy.wait_send()
 
 
 def hand_out(*refs):
-    count = len(refs) // 2
-    sems = refs[-1]
-    copies = [
-        pltpu.make_async_copy(refs[i], refs[count + i], sems.at[i]) for i in range(count)
-    ]
-    for copy in copies:
+    count = len(refs) // 3
+    takes, gives, slots, (into, out) = (
+        refs[:count],
+        refs[count : 2 * count],
+        refs[2 * count : 3 * count],
+        refs[3 * count :],
+    )
+    first = [pltpu.make_async_copy(takes[i], slots[i], into.at[i]) for i in range(count)]
+    second = [pltpu.make_async_copy(slots[i], gives[i], out.at[i]) for i in range(count)]
+    for copy in first:
         copy.start()
-    for copy in copies:
+    for copy, onward in zip(first, second):
+        copy.wait()
+        onward.start()
+    for copy in second:
         copy.wait()
 
 
 def local(blks, team, features, weight, bias, cotangent, adj_cols, adj_vals):
     block, width = features.shape
-    line = team // PLANE
     chunk = 8 * pl.cdiv(width, 8 * blks * team)
     f32, bf16 = jnp.float32, jnp.bfloat16
     dma = pltpu.SemaphoreType.DMA
@@ -381,15 +357,12 @@
         ((blks, block + 8, width), f32),
         ((blks, block, width), f32),
         ((blks, block + 8, width), f32),
-        ((blks, PLANE, line, chunk, width), f32),
-        ((blks, PLANE, line, chunk, width), f32),
-        ((PLANE, line, chunk, width), f32),
-        ((PLANE, line, chunk, width), f32),
-        ((line, chunk, width), f32),
-        ((line, chunk, width), f32),
-        ((blks, line, PLANE, chunk, width), f32),
+        ((blks, team, chunk, width), f32),
+        ((blks, team, chunk, width), f32),
+        ((team, chunk, width), f32),
+        ((team, chunk, width), f32),
+        ((blks, team, chunk, width), f32),
     ]
-    held = sum(math.prod(shape) * jnp.dtype(kind).itemsize for shape, kind in buffers)
     results = pl.pallas_call(
         functools.partial(kernel, blks, team),
         out_shape=outs,
@@ -402,7 +375,7 @@
         + [dma((team,))] * 4
         + [dma((blks,))] * 2,
         compiler_params=pltpu.CompilerParams(
-            collective_id=0, has_side_effects=True, vmem_limit_bytes=held + 12 * 2**20
+            collective_id=0, has_side_effects=True, vmem_limit_bytes=56 * 2**20
         ),
     )(features, weight, bias.reshape(1, width), cotangent, adj_cols, adj_vals)
     hidden, grad_input, grad_weight, grad_bias = pl.pallas_call(
@@ -410,7 +383,9 @@
         out_shape=outs,
         in_specs=[anywhere] * 4,
         out_specs=(anywhere,) * 4,
-        scratch_shapes=[dma((4,))],
+        scratch_shapes=[pltpu.VMEM(out.shape, out.dtype) for out in outs]
+        + [dma((4,)), dma((4,))],
+        compiler_params=pltpu.CompilerParams(vmem_limit_bytes=56 * 2**20),
     )(*results)
     return hidden, grad_input, grad_weight, grad_bias.reshape(width)
 

time: 70.5 us -> 46.6 us (0.66)
  Pallas kernels: 61.9 us -> 45.7 us
  local copies, waits for them, and re-layouts: 7.58 us -> 0 us
    pallas_call x1, Pallas kernels: 13.1 us -> 1.8 us  [local(): pl.pallas_call(hand_out, out_shape=outs, in_specs=[anywhere] * 4, out_spe...]
    unnamed x20 -> x0, local copies, waits for them, and re-layouts: 7.58 us -> none
    pallas_call x1, Pallas kernels: 48.9 us -> 43.9 us  [local(): pl.pallas_call(functools.partial(kernel, blks, team), out_shape=outs, in_...]
where the time goes in v3:
time: 46.6 us; the launch traced here: 46.4 us
  Pallas kernels  45.7 us (98%)
  between operations  0.64 us (1%)
    pallas_call x1, Pallas kernels, local(): pl.pallas_call(functools.partial(kernel, blks, team), out_shape=outs, in_...  43.9 us
    pallas_call x1, Pallas kernels, local(): pl.pallas_call(hand_out, out_shape=outs, in_specs=[anywhere] * 4, out_spe...  1.8 us

profile of v3, /device:TPU:0, one launch (start us, length us, event | category | flops | bytes accessed | tf_op | source)
XLA Modules:
  0.0 46.4 jit_solution(9227591500197680953)
XLA Ops:
  0.6 43.9 %shard_map.93 = (bf16[128,256]{1,0:T(8,128)(2,1)}, bf16[128,256]{1,0:T(8,128)(2,1)}, f32[256,256]{1,0:T(8,128)}, f32[1,256]{1,0:T(1,128)}) custom-call(bf16[128,256]{1,0:T(8,128)(2,1)} %x_ref.1, bf16[256,256]{1,0:T(8,128)(2,1)} %w_ref.1, f32[1,256]{1,0:T(1,128)} %bitcast.2, bf16[128,256]{1,0:T(8,128)(2,1)} %ct_ref.1, s32[1,2,1,12]{3,2,1,0:T(1,128)} %cols_ref.1, ...), custom_call_target="tpu_custom_call" | custom-call | tf_op jit(solution)/shard_map/pallas_call | solution.py:366
  44.6 1.8 %shard_map.94 = (bf16[128,256]{1,0:T(8,128)(2,1)}, bf16[128,256]{1,0:T(8,128)(2,1)}, f32[256,256]{1,0:T(8,128)}, f32[1,256]{1,0:T(1,128)}) custom-call(bf16[128,256]{1,0:T(8,128)(2,1)} %get-tuple-element.12.refs_0_, bf16[128,256]{1,0:T(8,128)(2,1)} %get-tuple-element.13.refs_1_, f32[256,256]{1,0:T(8,128)} %get-tuple-element.14.refs_2_, ...), custom_call_target="tpu_custom_call" | custom-call | tf_op jit(solution)/shard_map/pallas_call | solution.py:381

commit v4 on v3

--- a/solution.py
+++ b/solution.py
@@ -33,6 +33,10 @@
     gi_ref,
     gw_ref,
     gb_ref,
+    w_own,
+    b_own,
+    ct_own,
+    cols,
     vals,
     dense,
     xbuf,
@@ -46,7 +50,8 @@
     gtot,
     grs,
     gag,
-    vals_sem,
+    sums,
+    in_sem,
     x_send,
     x_recv,
     x_send2,
@@ -74,10 +79,8 @@
     width = x_ref.shape[1]
     nnz = vals_ref.shape[3]
     half = block // 2
+    line = team // PLANE
     fars = list(range(PLANE, team, PLANE))
-
-    fetch = pltpu.make_async_copy(vals_ref, vals, vals_sem)
-    fetch.start()
 
     barrier = pltpu.get_barrier_semaphore()
     partners = list(range(1, PLANE)) + fars
@@ -90,28 +93,50 @@
             barrier, inc=1, device_id=(flip(g, mask), m), device_id_type=MESH
         )
 
-    def rows_of(index, start=0, size=block):
-        return pl.ds(pl.multiple_of(index * block + start, half), size)
-
-    xbuf[rows_of(m), :] = x_ref[...]
-    fetch.wait()
-
-    def lay(c, carry):
+    def place(mask):
+        return (mask % PLANE) * line + mask // PLANE
+
+    def rows_of(mask, start=0, size=block):
+        first = place(mask) * block + start
+        return pl.ds(first, size)
+
+    fetches = [
+        pltpu.make_async_copy(src, dst, in_sem.at[i])
+        for i, (src, dst) in enumerate(
+            (
+                (x_ref, xbuf.at[rows_of(0)]),
+                (cols_ref, cols),
+                (vals_ref, vals),
+                (w_ref, w_own),
+                (b_ref, b_own),
+                (ct_ref, ct_own),
+            )
+        )
+    ]
+    for fetch in fetches:
+        fetch.start()
+
+    def lay(i, carry):
+        mask = (i % line) * PLANE + i // line
+        c = 0
+        bit = 1
+        while bit < team:
+            c = c + bit * ((m // bit + mask // bit) % 2)
+            bit *= 2
         for r in range(blks):
             slot = 0
             found = 0
             for k in range(nnz):
-                hit = cols_ref[0, r, 0, k] == c
+                hit = cols[0, r, 0, k] == c
                 slot = jnp.where(hit, k, slot)
                 found = jnp.where(hit, 1, found)
             keep = found.astype(jnp.float32)
             item = vals[0, r, 0, slot].astype(jnp.float32) * keep
-            span = pl.ds(pl.multiple_of(c * block, block), block)
+            span = pl.ds(pl.multiple_of(i * block, block), block)
             dense[r * block : (r + 1) * block, span] = item.astype(jnp.bfloat16)
         return carry
 
-    lax.fori_loop(0, team // 4, lay, 0)
-    dense[blks * block :, :] = jnp.ones((16, team * block), jnp.bfloat16)
+    fetches[0].wait()
     pl.semaphore_wait(barrier, len(partners) + blks - 1)
 
     pending = []
@@ -145,20 +170,31 @@
             self.sems2 = (sends2, recvs2)
 
         def item(self, mask):
-            return self.buf.at[rows_of(flip(m, mask))]
+            return self.buf.at[rows_of(mask)]
 
         def spread(self, far):
             for near in (1, 2):
-                item = self.item(far)
+                mask = far + near
                 sends, recvs = self.sems
-                send(item, item, sends.at[far + near], recvs.at[far + near], (g, flip(m, near)))
+                send(
+                    self.item(far),
+                    self.item(mask),
+                    sends.at[mask],
+                    recvs.at[mask],
+                    (g, flip(m, near)),
+                )
 
         def open(self):
-            self.spread(0)
             sends, recvs = self.sems
             for far in fars:
-                item = self.item(0)
-                send(item, item, sends.at[far], recvs.at[far], (g, flip(m, far)))
+                send(
+                    self.item(0),
+                    self.item(far),
+                    sends.at[far],
+                    recvs.at[far],
+                    (g, flip(m, far)),
+                )
+            self.spread(0)
 
         def wait(self, mask):
             sends, recvs = self.sems
@@ -169,17 +205,22 @@
             self.spread(far)
 
         def cross(self, far):
+            mask = far + 3
             for near, sems, start in ((1, self.sems, 0), (2, self.sems2, half)):
                 self.wait(far + near)
-                item = self.buf.at[rows_of(flip(m, far + near), start, half)]
-                mask = far + 3
-                send(item, item, sems[0].at[mask], sems[1].at[mask], (g, flip(m, 3 - near)))
+                send(
+                    self.buf.at[rows_of(far + near, start, half)],
+                    self.buf.at[rows_of(mask, start, half)],
+                    sems[0].at[mask],
+                    sems[1].at[mask],
+                    (g, flip(m, 3 - near)),
+                )
 
         def close(self):
             for far in [0] + fars:
                 mask = far + 3
                 for sems, start in ((self.sems, 0), (self.sems2, half)):
-                    item = self.buf.at[rows_of(flip(m, mask), start, half)]
+                    item = self.buf.at[rows_of(mask, start, half)]
                     arrived(item, sems[0].at[mask], sems[1].at[mask])
 
     def exchange(src_of, buf, send_sems, recv_sems):
@@ -191,40 +232,47 @@
         for mask in range(1, blks):
             arrived(buf.at[flip(g, mask)], send_sems.at[mask], recv_sems.at[mask])
 
-    deep = min(8, team) * block
-
-    def aggregate(buf, top, tall):
-        def term(span):
-            return jnp.dot(
+    deep = line * block
+    tall = min(2, blks) * block
+
+    def gain(buf, near, out):
+        span = slice(near * deep, (near + 1) * deep)
+        for top in range(0, blks * block, tall):
+            term = jnp.dot(
                 dense[top : top + tall, span],
                 buf[span, :],
                 preferred_element_type=jnp.float32,
+            ).reshape(tall // block, block, width)
+            groups = pl.ds(top // block, tall // block)
+            if near == 0:
+                out[groups, :block] = term
+            else:
+                out[groups, :block] += term
+
+    def tally(near):
+        for far in [0] + fars:
+            mask = near + far
+            sums[flip(m, mask)] = jnp.sum(
+                pbuf[rows_of(mask), :].astype(jnp.float32).reshape(block // 8, 8, width),
+                axis=0,
             )
-
-        if team * block <= 2 * deep:
-            return sum(term(slice(i, i + deep)) for i in range(0, team * block, deep))
-
-        def step(i, total):
-            return total + term(pl.ds(pl.multiple_of(i * deep, deep), deep))
-
-        start = jnp.zeros((tall, width), jnp.float32)
-        return lax.fori_loop(0, team * block // deep, step, start)
-
-    tall = min(2, blks) * block
 
     xs = Gather(xbuf, x_send, x_recv, x_send2, x_recv2)
     xs.open()
-    lax.fori_loop(team // 4, team // 2, lay, 0)
-    for place, far in enumerate(fars):
+    for fetch in fetches[1:]:
+        fetch.wait()
+    lax.fori_loop(0, line, lay, 0)
+    for far in fars:
         xs.forward(far)
         xs.cross(far - PLANE)
-    lax.fori_loop(team // 2, team, lay, 0)
+    lax.fori_loop(line, 2 * line, lay, 0)
+    gain(xbuf, 0, part)
     xs.cross(fars[-1])
+    lax.fori_loop(2 * line, 4 * line, lay, 0)
+    gain(xbuf, 1, part)
+    gain(xbuf, 2, part)
     xs.close()
-    for top in range(0, blks * block, tall):
-        part[pl.ds(top // block, tall // block)] = aggregate(xbuf, top, tall).reshape(
-            tall // block, block, width
-        )
+    gain(xbuf, 3, part)
     exchange(lambda peer: part.at[peer], ybuf, y_send, y_recv)
     y = part[g]
     exchanged(ybuf, y_send, y_recv)
@@ -232,11 +280,11 @@
         y = y + ybuf[flip(g, mask)]
     high = y.astype(jnp.bfloat16)
     low = (y - high.astype(jnp.float32)).astype(jnp.bfloat16)
-    weight = w_ref[...]
+    weight = w_own[...]
     pre = (
         jnp.dot(high, weight, preferred_element_type=jnp.float32)
         + jnp.dot(low, weight, preferred_element_type=jnp.float32)
-        + b_ref[...]
+        + b_own[...]
     )
     square = pre * pre
     bent = jnp.tanh(0.7978845608 * (pre + 0.044715 * (square * pre)))
@@ -244,9 +292,11 @@
     slope = gate + (0.5 * pre) * ((1.0 - bent) * (1.0 + bent)) * (
         0.7978845608 * (1.0 + 0.134145 * square)
     )
-    pulled = (ct_ref[...].astype(jnp.float32) * slope).astype(jnp.bfloat16)
-
-    pbuf[rows_of(m), :] = pulled
+    pulled = (ct_own[...].astype(jnp.float32) * slope).astype(jnp.bfloat16)
+
+    pbuf[rows_of(0), :] = pulled
+    forward_sends = pending[:]
+    del pending[:]
     ps = Gather(pbuf, p_send, p_recv, p_send2, p_recv2)
     ps.open()
     turned = (((0,), (0,)), ((), ()))
@@ -284,20 +334,28 @@
     for mask in range(1, team):
         item = gag.at[g, m]
         send(item, item, ag_send.at[mask], ag_recv.at[mask], (g, flip(m, mask)))
+    for copy in forward_sends:
+        copy.wait_send()
+    gain(pbuf, 0, back)
+    tally(0)
     ps.cross(fars[-1])
+    gain(pbuf, 1, back)
+    gain(pbuf, 2, back)
+    tally(1)
+    tally(2)
     ps.close()
-    for top in range(0, blks * block, tall):
-        extra = 16 if top + tall == blks * block else 0
-        total = aggregate(pbuf, top, tall + extra)
-        back[pl.ds(top // block, tall // block), :block] = total[:tall].reshape(
-            tall // block, block, width
-        )
+    gain(pbuf, 3, back)
+    tally(3)
     for r in range(blks):
-        back[r, block:] = total[tall : tall + 8]
+        back[r, block:] = jnp.sum(sums[...], axis=0)
+    earlier = pending[:]
+    del pending[:]
     exchange(lambda peer: back.at[peer], sbuf, s_send, s_recv)
     for mask in range(1, team):
         arrived(gag.at[g, flip(m, mask)], ag_send.at[mask], ag_recv.at[mask])
     exchange(lambda peer: gag.at[g], gag, l4_send, l4_recv)
+    for copy in earlier:
+        copy.wait_send()
     spread = back[g]
     exchanged(sbuf, s_send, s_recv)
     for mask in range(1, blks):
@@ -308,7 +366,7 @@
         (((1,), (1,)), ((), ())),
         preferred_element_type=jnp.float32,
     ).astype(jnp.bfloat16)
-    gb_ref[...] = spread[block : block + 1]
+    gb_ref[...] = jnp.sum(spread[block:], axis=0, keepdims=True)
     exchanged(gag, l4_send, l4_recv)
     gw_ref[...] = gag[...].reshape(chunks * chunk, width)[:width]
     for copy in pending:
@@ -349,8 +407,11 @@
         jax.ShapeDtypeStruct((1, width), f32),
     )
     buffers = [
+        ((width, width), bf16),
+        ((1, width), f32),
+        ((block, width), bf16),
         (adj_vals.shape, bf16),
-        ((panels + 16, team * block), bf16),
+        ((panels, team * block), bf16),
         ((team * block, width), bf16),
         ((team * block, width), bf16),
         ((blks, block, width), f32),
@@ -362,14 +423,17 @@
         ((team, chunk, width), f32),
         ((team, chunk, width), f32),
         ((blks, team, chunk, width), f32),
+        ((team, 8, width), f32),
     ]
     results = pl.pallas_call(
         functools.partial(kernel, blks, team),
         out_shape=outs,
-        in_specs=[vmem, vmem, vmem, vmem, pl.BlockSpec(memory_space=pltpu.SMEM), anywhere],
+        in_specs=[anywhere] * 6,
         out_specs=(vmem,) * 4,
-        scratch_shapes=[pltpu.VMEM(shape, kind) for shape, kind in buffers]
-        + [dma]
+        scratch_shapes=[pltpu.VMEM(shape, kind) for shape, kind in buffers[:3]]
+        + [pltpu.SMEM(adj_cols.shape, jnp.int32)]
+        + [pltpu.VMEM(shape, kind) for shape, kind in buffers[3:]]
+        + [dma((6,))]
         + [dma((team,))] * 8
         + [dma((blks,))] * 6
         + [dma((team,))] * 4

time: 46.6 us -> 44.8 us (0.961)
  Pallas kernels: 45.7 us -> 44 us
    pallas_call x1, Pallas kernels: 43.9 us -> 42.2 us  [local(): pl.pallas_call(functools.partial(kernel, blks, team), out_shape=outs, in_...]
where the time goes in v4:
time: 44.8 us; the launch traced here: 44.6 us
  Pallas kernels  44 us (98%)
  between operations  0.64 us (1%)
    pallas_call x1, Pallas kernels, local(): pl.pallas_call(functools.partial(kernel, blks, team), out_shape=outs, in_...  42.2 us
    pallas_call x1, Pallas kernels, local(): pl.pallas_call(hand_out, out_shape=outs, in_specs=[anywhere] * 4, out_spe...  1.8 us

profile of v4, /device:TPU:0, one launch (start us, length us, event | category | flops | bytes accessed | tf_op | source)
XLA Modules:
  0.0 44.6 jit_solution(5011445358035352982)
XLA Ops:
  0.6 42.2 %shard_map.93 = (bf16[128,256]{1,0:T(8,128)(2,1)}, bf16[128,256]{1,0:T(8,128)(2,1)}, f32[256,256]{1,0:T(8,128)}, f32[1,256]{1,0:T(1,128)}) custom-call(bf16[128,256]{1,0:T(8,128)(2,1)} %x_ref.1, bf16[256,256]{1,0:T(8,128)(2,1)} %w_ref.1, f32[1,256]{1,0:T(1,128)} %bitcast.2, bf16[128,256]{1,0:T(8,128)(2,1)} %ct_ref.1, s32[1,2,1,12]{3,2,1,0:T(1,128)} %cols_ref.1, ...), custom_call_target="tpu_custom_call" | custom-call | tf_op jit(solution)/shard_map/pallas_call | solution.py:428
  42.8 1.8 %shard_map.94 = (bf16[128,256]{1,0:T(8,128)(2,1)}, bf16[128,256]{1,0:T(8,128)(2,1)}, f32[256,256]{1,0:T(8,128)}, f32[1,256]{1,0:T(1,128)}) custom-call(bf16[128,256]{1,0:T(8,128)(2,1)} %get-tuple-element.12.refs_0_, bf16[128,256]{1,0:T(8,128)(2,1)} %get-tuple-element.13.refs_1_, f32[256,256]{1,0:T(8,128)} %get-tuple-element.14.refs_2_, ...), custom_call_target="tpu_custom_call" | custom-call | tf_op jit(solution)/shard_map/pallas_call | solution.py:445

commit v5 on v4

--- a/solution.py
+++ b/solution.py
@@ -80,31 +80,44 @@
     nnz = vals_ref.shape[3]
     half = block // 2
     line = team // PLANE
-    fars = list(range(PLANE, team, PLANE))
+    z = m // PLANE
+    last = line - 1
 
     barrier = pltpu.get_barrier_semaphore()
-    partners = list(range(1, PLANE)) + fars
-    for mask in partners:
-        pl.semaphore_signal(
-            barrier, inc=1, device_id=(g, flip(m, mask)), device_id_type=MESH
-        )
+
+    def greet(device):
+        pl.semaphore_signal(barrier, inc=1, device_id=device, device_id_type=MESH)
+
+    pl.when(z < last)(lambda: greet((g, m + PLANE)))
+    pl.when(z > 0)(lambda: greet((g, m - PLANE)))
+    for near in (1, 2):
+        greet((g, flip(m, near)))
     for mask in range(1, blks):
-        pl.semaphore_signal(
-            barrier, inc=1, device_id=(flip(g, mask), m), device_id_type=MESH
-        )
-
-    def place(mask):
-        return (mask % PLANE) * line + mask // PLANE
-
-    def rows_of(mask, start=0, size=block):
-        first = place(mask) * block + start
+        greet((flip(g, mask), m))
+
+    def rows_of(near, k, start=0, size=block):
+        first = (near * line + k) * block + start
+        if not isinstance(first, int):
+            first = pl.multiple_of(first, half)
         return pl.ds(first, size)
+
+    def owner(near, k):
+        return flip((z + k) % line * PLANE + m % PLANE, near)
+
+    def nth(n):
+        both = jnp.minimum(z, last - z)
+        paired = n <= 2 * both
+        distance = jnp.where(paired, (n + 1) // 2, n - both)
+        above = jnp.where(paired, n % 2 == 1, z < last - z)
+        return jnp.where(above, distance, line - distance)
+
+    order = [0] + [nth(n) for n in range(1, line)]
 
     fetches = [
         pltpu.make_async_copy(src, dst, in_sem.at[i])
         for i, (src, dst) in enumerate(
             (
-                (x_ref, xbuf.at[rows_of(0)]),
+                (x_ref, xbuf.at[rows_of(0, 0)]),
                 (cols_ref, cols),
                 (vals_ref, vals),
                 (w_ref, w_own),
@@ -117,12 +130,10 @@
         fetch.start()
 
     def lay(i, carry):
-        mask = (i % line) * PLANE + i // line
-        c = 0
-        bit = 1
-        while bit < team:
-            c = c + bit * ((m // bit + mask // bit) % 2)
-            bit *= 2
+        near = i // line
+        near1, near2 = near % 2, near // 2
+        p1, p2 = m % 2, m // 2 % 2
+        c = (z + i) % line * PLANE + (p2 + near2) % 2 * 2 + (p1 + near1) % 2
         for r in range(blks):
             slot = 0
             found = 0
@@ -137,11 +148,13 @@
         return carry
 
     fetches[0].wait()
-    pl.semaphore_wait(barrier, len(partners) + blks - 1)
+    pl.semaphore_wait(
+        barrier, 1 + blks + (z < last).astype(jnp.int32) + (z > 0).astype(jnp.int32)
+    )
 
     pending = []
 
-    def send(src, dst, send_sem, recv_sem, device):
+    def send(src, dst, send_sem, recv_sem, device, when=None):
         copy = pltpu.make_async_remote_copy(
             src_ref=src,
             dst_ref=dst,
@@ -150,8 +163,18 @@
             device_id=device,
             device_id_type=MESH,
         )
-        copy.start()
-        pending.append(copy)
+        if when is None:
+            copy.start()
+        else:
+            pl.when(when)(copy.start)
+        pending.append((copy, when))
+
+    def sent(copies):
+        for copy, when in copies:
+            if when is None:
+                copy.wait_send()
+            else:
+                pl.when(when)(copy.wait_send)
 
     def arrived(dst, send_sem, recv_sem):
         pltpu.make_async_remote_copy(
@@ -169,59 +192,65 @@
             self.sems = (sends, recvs)
             self.sems2 = (sends2, recvs2)
 
-        def item(self, mask):
-            return self.buf.at[rows_of(mask)]
-
-        def spread(self, far):
+        def item(self, near, k):
+            return self.buf.at[rows_of(near, k)]
+
+        def move(self, k, to, device, when, send_sem):
+            recvs = self.sems[1]
+            send(self.item(0, k), self.item(0, to), send_sem, recvs.at[to], device, when)
+
+        def spread(self, k):
+            sends, recvs = self.sems
             for near in (1, 2):
-                mask = far + near
-                sends, recvs = self.sems
+                at = near * line + k
                 send(
-                    self.item(far),
-                    self.item(mask),
-                    sends.at[mask],
-                    recvs.at[mask],
+                    self.item(0, k),
+                    self.item(near, k),
+                    sends.at[at],
+                    recvs.at[at],
                     (g, flip(m, near)),
                 )
 
         def open(self):
+            sends, sends2 = self.sems[0], self.sems2[0]
+            self.move(0, last, (g, m + PLANE), z < last, sends.at[0])
+            self.move(0, 1 % line, (g, m - PLANE), z > 0, sends2.at[0])
+            self.spread(0)
+
+        def wait(self, near, k):
             sends, recvs = self.sems
-            for far in fars:
+            at = near * line + k
+            arrived(self.item(near, k), sends.at[at], recvs.at[at])
+
+        def forward(self, n):
+            k = order[n]
+            sends, sends2 = self.sems[0], self.sems2[0]
+            self.wait(0, k)
+            down = jnp.logical_and(z + k < line, z > 0)
+            up = jnp.logical_and(z + k >= line, z < last)
+            self.move(k, (k + 1) % line, (g, m - PLANE), down, sends.at[k])
+            self.move(k, (k - 1) % line, (g, m + PLANE), up, sends2.at[k])
+            self.spread(k)
+
+        def cross(self, n):
+            k = order[n]
+            at = 3 * line + k
+            for near, sems, start in ((1, self.sems, 0), (2, self.sems2, half)):
+                self.wait(near, k)
                 send(
-                    self.item(0),
-                    self.item(far),
-                    sends.at[far],
-                    recvs.at[far],
-                    (g, flip(m, far)),
-                )
-            self.spread(0)
-
-        def wait(self, mask):
-            sends, recvs = self.sems
-            arrived(self.item(mask), sends.at[mask], recvs.at[mask])
-
-        def forward(self, far):
-            self.wait(far)
-            self.spread(far)
-
-        def cross(self, far):
-            mask = far + 3
-            for near, sems, start in ((1, self.sems, 0), (2, self.sems2, half)):
-                self.wait(far + near)
-                send(
-                    self.buf.at[rows_of(far + near, start, half)],
-                    self.buf.at[rows_of(mask, start, half)],
-                    sems[0].at[mask],
-                    sems[1].at[mask],
+                    self.buf.at[rows_of(near, k, start, half)],
+                    self.buf.at[rows_of(3, k, start, half)],
+                    sems[0].at[at],
+                    sems[1].at[at],
                     (g, flip(m, 3 - near)),
                 )
 
         def close(self):
-            for far in [0] + fars:
-                mask = far + 3
+            for k in range(line):
+                at = 3 * line + k
                 for sems, start in ((self.sems, 0), (self.sems2, half)):
-                    item = self.buf.at[rows_of(mask, start, half)]
-                    arrived(item, sems[0].at[mask], sems[1].at[mask])
+                    item = self.buf.at[rows_of(3, k, start, half)]
+                    arrived(item, sems[0].at[at], sems[1].at[at])
 
     def exchange(src_of, buf, send_sems, recv_sems):
         for mask in range(1, blks):
@@ -250,10 +279,9 @@
                 out[groups, :block] += term
 
     def tally(near):
-        for far in [0] + fars:
-            mask = near + far
-            sums[flip(m, mask)] = jnp.sum(
-                pbuf[rows_of(mask), :].astype(jnp.float32).reshape(block // 8, 8, width),
+        for k in range(line):
+            sums[owner(near, k)] = jnp.sum(
+                pbuf[rows_of(near, k), :].astype(jnp.float32).reshape(block // 8, 8, width),
                 axis=0,
             )
 
@@ -262,12 +290,12 @@
     for fetch in fetches[1:]:
         fetch.wait()
     lax.fori_loop(0, line, lay, 0)
-    for far in fars:
-        xs.forward(far)
-        xs.cross(far - PLANE)
+    for n in range(1, line):
+        xs.forward(n)
+        xs.cross(n - 1)
     lax.fori_loop(line, 2 * line, lay, 0)
     gain(xbuf, 0, part)
-    xs.cross(fars[-1])
+    xs.cross(last)
     lax.fori_loop(2 * line, 4 * line, lay, 0)
     gain(xbuf, 1, part)
     gain(xbuf, 2, part)
@@ -294,7 +322,7 @@
     )
     pulled = (ct_own[...].astype(jnp.float32) * slope).astype(jnp.bfloat16)
 
-    pbuf[rows_of(0), :] = pulled
+    pbuf[rows_of(0, 0), :] = pulled
     forward_sends = pending[:]
     del pending[:]
     ps = Gather(pbuf, p_send, p_recv, p_send2, p_recv2)
@@ -311,7 +339,7 @@
         whole = jnp.concatenate([whole, empty], axis=0)
     gpart[...] = whole.reshape(blks, team, chunk, width)
     exchange(lambda peer: gpart.at[peer], gl1, l1_send, l1_recv)
-    ps.forward(fars[0])
+    ps.forward(1)
 
     exchanged(gl1, l1_send, l1_recv)
     total = gpart[g]
@@ -325,20 +353,19 @@
     hidden_ref[...] = (pre * gate).astype(jnp.bfloat16)
 
     ps.cross(0)
-    for far in fars[1:]:
-        ps.forward(far)
-        ps.cross(far - PLANE)
+    for n in range(2, line):
+        ps.forward(n)
+        ps.cross(n - 1)
     for mask in range(1, team):
         arrived(grs.at[flip(m, mask)], rs_send.at[mask], rs_recv.at[mask])
     gag[g, m] = jnp.sum(grs[...], axis=0)
     for mask in range(1, team):
         item = gag.at[g, m]
         send(item, item, ag_send.at[mask], ag_recv.at[mask], (g, flip(m, mask)))
-    for copy in forward_sends:
-        copy.wait_send()
+    sent(forward_sends)
     gain(pbuf, 0, back)
     tally(0)
-    ps.cross(fars[-1])
+    ps.cross(last)
     gain(pbuf, 1, back)
     gain(pbuf, 2, back)
     tally(1)
@@ -354,8 +381,7 @@
     for mask in range(1, team):
         arrived(gag.at[g, flip(m, mask)], ag_send.at[mask], ag_recv.at[mask])
     exchange(lambda peer: gag.at[g], gag, l4_send, l4_recv)
-    for copy in earlier:
-        copy.wait_send()
+    sent(earlier)
     spread = back[g]
     exchanged(sbuf, s_send, s_recv)
     for mask in range(1, blks):
@@ -369,8 +395,7 @@
     gb_ref[...] = jnp.sum(spread[block:], axis=0, keepdims=True)
     exchanged(gag, l4_send, l4_recv)
     gw_ref[...] = gag[...].reshape(chunks * chunk, width)[:width]
-    for copy in pending:
-        copy.wait_send()
+    sent(pending)
 
 
 def hand_out(*refs):

time: 44.8 us -> 47.3 us (1.056)
  Pallas kernels: 44 us -> 46.5 us
    pallas_call x1, Pallas kernels: 42.2 us -> 44.7 us  [local(): pl.pallas_call(functools.partial(kernel, blks, team), out_shape=outs, in_...]
where the time goes in v5:
time: 47.3 us; the launch traced here: 47.1 us
  Pallas kernels  46.5 us (98%)
  between operations  0.64 us (1%)
    pallas_call x1, Pallas kernels, local(): pl.pallas_call(functools.partial(kernel, blks, team), out_shape=outs, in_...  44.7 us
    pallas_call x1, Pallas kernels, local(): pl.pallas_call(hand_out, out_shape=outs, in_specs=[anywhere] * 4, out_spe...  1.8 us

profile of v5, /device:TPU:0, one launch (start us, length us, event | category | flops | bytes accessed | tf_op | source)
XLA Modules:
  0.0 47.1 jit_solution(2541522952384563646)
XLA Ops:
  0.6 44.7 %shard_map.93 = (bf16[128,256]{1,0:T(8,128)(2,1)}, bf16[128,256]{1,0:T(8,128)(2,1)}, f32[256,256]{1,0:T(8,128)}, f32[1,256]{1,0:T(1,128)}) custom-call(bf16[128,256]{1,0:T(8,128)(2,1)} %x_ref.1, bf16[256,256]{1,0:T(8,128)(2,1)} %w_ref.1, f32[1,256]{1,0:T(1,128)} %bitcast.2, bf16[128,256]{1,0:T(8,128)(2,1)} %ct_ref.1, s32[1,2,1,12]{3,2,1,0:T(1,128)} %cols_ref.1, ...), custom_call_target="tpu_custom_call" | custom-call | tf_op jit(solution)/shard_map/pallas_call | solution.py:453
  45.3 1.8 %shard_map.94 = (bf16[128,256]{1,0:T(8,128)(2,1)}, bf16[128,256]{1,0:T(8,128)(2,1)}, f32[256,256]{1,0:T(8,128)}, f32[1,256]{1,0:T(1,128)}) custom-call(bf16[128,256]{1,0:T(8,128)(2,1)} %get-tuple-element.12.refs_0_, bf16[128,256]{1,0:T(8,128)(2,1)} %get-tuple-element.13.refs_1_, f32[256,256]{1,0:T(8,128)} %get-tuple-element.14.refs_2_, ...), custom_call_target="tpu_custom_call" | custom-call | tf_op jit(solution)/shard_map/pallas_call | solution.py:470

commit v6 on v4

--- a/solution.py
+++ b/solution.py
@@ -54,12 +54,8 @@
     in_sem,
     x_send,
     x_recv,
-    x_send2,
-    x_recv2,
     p_send,
     p_recv,
-    p_send2,
-    p_recv2,
     y_send,
     y_recv,
     s_send,
@@ -78,7 +74,6 @@
     block = x_ref.shape[0]
     width = x_ref.shape[1]
     nnz = vals_ref.shape[3]
-    half = block // 2
     line = team // PLANE
     fars = list(range(PLANE, team, PLANE))
 
@@ -96,9 +91,8 @@
     def place(mask):
         return (mask % PLANE) * line + mask // PLANE
 
-    def rows_of(mask, start=0, size=block):
-        first = place(mask) * block + start
-        return pl.ds(first, size)
+    def rows_of(mask):
+        return pl.ds(place(mask) * block, block)
 
     fetches = [
         pltpu.make_async_copy(src, dst, in_sem.at[i])
@@ -164,16 +158,15 @@
         ).wait_recv()
 
     class Gather:
-        def __init__(self, buf, sends, recvs, sends2, recvs2):
+        def __init__(self, buf, sends, recvs):
             self.buf = buf
             self.sems = (sends, recvs)
-            self.sems2 = (sends2, recvs2)
 
         def item(self, mask):
             return self.buf.at[rows_of(mask)]
 
         def spread(self, far):
-            for near in (1, 2):
+            for near in (3, 1, 2):
                 mask = far + near
                 sends, recvs = self.sems
                 send(
@@ -204,24 +197,9 @@
             self.wait(far)
             self.spread(far)
 
-        def cross(self, far):
-            mask = far + 3
-            for near, sems, start in ((1, self.sems, 0), (2, self.sems2, half)):
+        def close(self, near):
+            for far in [0] + fars:
                 self.wait(far + near)
-                send(
-                    self.buf.at[rows_of(far + near, start, half)],
-                    self.buf.at[rows_of(mask, start, half)],
-                    sems[0].at[mask],
-                    sems[1].at[mask],
-                    (g, flip(m, 3 - near)),
-                )
-
-        def close(self):
-            for far in [0] + fars:
-                mask = far + 3
-                for sems, start in ((self.sems, 0), (self.sems2, half)):
-                    item = self.buf.at[rows_of(mask, start, half)]
-                    arrived(item, sems[0].at[mask], sems[1].at[mask])
 
     def exchange(src_of, buf, send_sems, recv_sems):
         for mask in range(1, blks):
@@ -257,22 +235,18 @@
                 axis=0,
             )
 
-    xs = Gather(xbuf, x_send, x_recv, x_send2, x_recv2)
+    xs = Gather(xbuf, x_send, x_recv)
     xs.open()
     for fetch in fetches[1:]:
         fetch.wait()
     lax.fori_loop(0, line, lay, 0)
     for far in fars:
         xs.forward(far)
-        xs.cross(far - PLANE)
-    lax.fori_loop(line, 2 * line, lay, 0)
-    gain(xbuf, 0, part)
-    xs.cross(fars[-1])
-    lax.fori_loop(2 * line, 4 * line, lay, 0)
-    gain(xbuf, 1, part)
-    gain(xbuf, 2, part)
-    xs.close()
-    gain(xbuf, 3, part)
+    lax.fori_loop(line, 4 * line, lay, 0)
+    for near in range(PLANE):
+        if near:
+            xs.close(near)
+        gain(xbuf, near, part)
     exchange(lambda peer: part.at[peer], ybuf, y_send, y_recv)
     y = part[g]
     exchanged(ybuf, y_send, y_recv)
@@ -297,7 +271,7 @@
     pbuf[rows_of(0), :] = pulled
     forward_sends = pending[:]
     del pending[:]
-    ps = Gather(pbuf, p_send, p_recv, p_send2, p_recv2)
+    ps = Gather(pbuf, p_send, p_recv)
     ps.open()
     turned = (((0,), (0,)), ((), ()))
     grad = lax.dot_general(high, pulled, turned, preferred_element_type=jnp.float32)
@@ -324,10 +298,8 @@
     grs[m] = gtot[m]
     hidden_ref[...] = (pre * gate).astype(jnp.bfloat16)
 
-    ps.cross(0)
     for far in fars[1:]:
         ps.forward(far)
-        ps.cross(far - PLANE)
     for mask in range(1, team):
         arrived(grs.at[flip(m, mask)], rs_send.at[mask], rs_recv.at[mask])
     gag[g, m] = jnp.sum(grs[...], axis=0)
@@ -336,16 +308,11 @@
         send(item, item, ag_send.at[mask], ag_recv.at[mask], (g, flip(m, mask)))
     for copy in forward_sends:
         copy.wait_send()
-    gain(pbuf, 0, back)
-    tally(0)
-    ps.cross(fars[-1])
-    gain(pbuf, 1, back)
-    gain(pbuf, 2, back)
-    tally(1)
-    tally(2)
-    ps.close()
-    gain(pbuf, 3, back)
-    tally(3)
+    for near in range(PLANE):
+        if near:
+            ps.close(near)
+        gain(pbuf, near, back)
+        tally(near)
     for r in range(blks):
         back[r, block:] = jnp.sum(sums[...], axis=0)
     earlier = pending[:]
@@ -434,7 +401,7 @@
         + [pltpu.SMEM(adj_cols.shape, jnp.int32)]
         + [pltpu.VMEM(shape, kind) for shape, kind in buffers[3:]]
         + [dma((6,))]
-        + [dma((team,))] * 8
+        + [dma((team,))] * 4
         + [dma((blks,))] * 6
         + [dma((team,))] * 4
         + [dma((blks,))] * 2,

time: 44.8 us -> 44.3 us (0.989)
  Pallas kernels: 44 us -> 43.5 us
    pallas_call x1, Pallas kernels: 42.2 us -> 41.7 us  [local(): pl.pallas_call(functools.partial(kernel, blks, team), out_shape=outs, in_...]
where the time goes in v6:
time: 44.3 us; the launch traced here: 44.1 us
  Pallas kernels  43.5 us (98%)
  between operations  0.64 us (1%)
    pallas_call x1, Pallas kernels, local(): pl.pallas_call(functools.partial(kernel, blks, team), out_shape=outs, in_...  41.7 us
    pallas_call x1, Pallas kernels, local(): pl.pallas_call(hand_out, out_shape=outs, in_specs=[anywhere] * 4, out_spe...  1.8 us

profile of v6, /device:TPU:0, one launch (start us, length us, event | category | flops | bytes accessed | tf_op | source)
XLA Modules:
  0.0 44.1 jit_solution(1179855946435006277)
XLA Ops:
  0.6 41.7 %shard_map.93 = (bf16[128,256]{1,0:T(8,128)(2,1)}, bf16[128,256]{1,0:T(8,128)(2,1)}, f32[256,256]{1,0:T(8,128)}, f32[1,256]{1,0:T(1,128)}) custom-call(bf16[128,256]{1,0:T(8,128)(2,1)} %x_ref.1, bf16[256,256]{1,0:T(8,128)(2,1)} %w_ref.1, f32[1,256]{1,0:T(1,128)} %bitcast.2, bf16[128,256]{1,0:T(8,128)(2,1)} %ct_ref.1, s32[1,2,1,12]{3,2,1,0:T(1,128)} %cols_ref.1, ...), custom_call_target="tpu_custom_call" | custom-call | tf_op jit(solution)/shard_map/pallas_call | solution.py:395
  42.3 1.8 %shard_map.94 = (bf16[128,256]{1,0:T(8,128)(2,1)}, bf16[128,256]{1,0:T(8,128)(2,1)}, f32[256,256]{1,0:T(8,128)}, f32[1,256]{1,0:T(1,128)}) custom-call(bf16[128,256]{1,0:T(8,128)(2,1)} %get-tuple-element.12.refs_0_, bf16[128,256]{1,0:T(8,128)(2,1)} %get-tuple-element.13.refs_1_, f32[256,256]{1,0:T(8,128)} %get-tuple-element.14.refs_2_, ...), custom_call_target="tpu_custom_call" | custom-call | tf_op jit(solution)/shard_map/pallas_call | solution.py:412

commit v7 on v4

--- a/solution.py
+++ b/solution.py
@@ -81,6 +81,7 @@
     half = block // 2
     line = team // PLANE
     fars = list(range(PLANE, team, PLANE))
+    early = list(range(0, team // 2, PLANE))
 
     barrier = pltpu.get_barrier_semaphore()
     partners = list(range(1, PLANE)) + fars
@@ -173,7 +174,7 @@
             return self.buf.at[rows_of(mask)]
 
         def spread(self, far):
-            for near in (1, 2):
+            for near in (1, 2) if far in early else (3, 1, 2):
                 mask = far + near
                 sends, recvs = self.sems
                 send(
@@ -208,6 +209,8 @@
             mask = far + 3
             for near, sems, start in ((1, self.sems, 0), (2, self.sems2, half)):
                 self.wait(far + near)
+                if far not in early:
+                    continue
                 send(
                     self.buf.at[rows_of(far + near, start, half)],
                     self.buf.at[rows_of(mask, start, half)],
@@ -219,6 +222,9 @@
         def close(self):
             for far in [0] + fars:
                 mask = far + 3
+                if far not in early:
+                    self.wait(mask)
+                    continue
                 for sems, start in ((self.sems, 0), (self.sems2, half)):
                     item = self.buf.at[rows_of(mask, start, half)]
                     arrived(item, sems[0].at[mask], sems[1].at[mask])
@@ -264,10 +270,13 @@
     lax.fori_loop(0, line, lay, 0)
     for far in fars:
         xs.forward(far)
-        xs.cross(far - PLANE)
+        if far - PLANE in early:
+            xs.cross(far - PLANE)
     lax.fori_loop(line, 2 * line, lay, 0)
     gain(xbuf, 0, part)
-    xs.cross(fars[-1])
+    for far in fars:
+        if far not in early:
+            xs.cross(far)
     lax.fori_loop(2 * line, 4 * line, lay, 0)
     gain(xbuf, 1, part)
     gain(xbuf, 2, part)
@@ -327,7 +336,8 @@
     ps.cross(0)
     for far in fars[1:]:
         ps.forward(far)
-        ps.cross(far - PLANE)
+        if far - PLANE in early:
+            ps.cross(far - PLANE)
     for mask in range(1, team):
         arrived(grs.at[flip(m, mask)], rs_send.at[mask], rs_recv.at[mask])
     gag[g, m] = jnp.sum(grs[...], axis=0)
@@ -338,7 +348,9 @@
         copy.wait_send()
     gain(pbuf, 0, back)
     tally(0)
-    ps.cross(fars[-1])
+    for far in fars:
+        if far not in early:
+            ps.cross(far)
     gain(pbuf, 1, back)
     gain(pbuf, 2, back)
     tally(1)

time: 44.8 us -> 45.1 us (level)
  no operation moved by 1% of the time
where the time goes in v7:
time: 45.1 us; the launch traced here: 44.9 us
  Pallas kernels  44.3 us (98%)
  between operations  0.64 us (1%)
    pallas_call x1, Pallas kernels, local(): pl.pallas_call(functools.partial(kernel, blks, team), out_shape=outs, in_...  42.5 us
    pallas_call x1, Pallas kernels, local(): pl.pallas_call(hand_out, out_shape=outs, in_specs=[anywhere] * 4, out_spe...  1.8 us

profile of v7, /device:TPU:0, one launch (start us, length us, event | category | flops | bytes accessed | tf_op | source)
XLA Modules:
  0.0 44.9 jit_solution(6582659732414545224)
XLA Ops:
  0.6 42.5 %shard_map.93 = (bf16[128,256]{1,0:T(8,128)(2,1)}, bf16[128,256]{1,0:T(8,128)(2,1)}, f32[256,256]{1,0:T(8,128)}, f32[1,256]{1,0:T(1,128)}) custom-call(bf16[128,256]{1,0:T(8,128)(2,1)} %x_ref.1, bf16[256,256]{1,0:T(8,128)(2,1)} %w_ref.1, f32[1,256]{1,0:T(1,128)} %bitcast.2, bf16[128,256]{1,0:T(8,128)(2,1)} %ct_ref.1, s32[1,2,1,12]{3,2,1,0:T(1,128)} %cols_ref.1, ...), custom_call_target="tpu_custom_call" | custom-call | tf_op jit(solution)/shard_map/pallas_call | solution.py:440
  43.1 1.8 %shard_map.94 = (bf16[128,256]{1,0:T(8,128)(2,1)}, bf16[128,256]{1,0:T(8,128)(2,1)}, f32[256,256]{1,0:T(8,128)}, f32[1,256]{1,0:T(1,128)}) custom-call(bf16[128,256]{1,0:T(8,128)(2,1)} %get-tuple-element.12.refs_0_, bf16[128,256]{1,0:T(8,128)(2,1)} %get-tuple-element.13.refs_1_, f32[256,256]{1,0:T(8,128)} %get-tuple-element.14.refs_2_, ...), custom_call_target="tpu_custom_call" | custom-call | tf_op jit(solution)/shard_map/pallas_call | solution.py:457
